TPU v7x, 32 devices: a whole 2x2x4 slice. The times are simulated.
32 devices in a mesh: seed: 4 (over y, x), tok: 8 (over z, core).
Axes of the slice: x: 2, y: 2, z: 4, core: 2. Of those that a mesh axis runs over, the one named last changes fastest.
Arguments:
- atom_feats: bfloat16 [8192, 8, 128], P('tok', 'seed'), may hold values from -6 to 6
- atom_index: int32 [8192], P('tok'), may hold values from 0 to 1023, as said below
- token_cond: bfloat16 [1024, 768], P('tok'), may hold values from -6 to 6
- pair_bias: bfloat16 [16, 1024, 1024], P('seed', 'tok'), may hold values from -8 to 248
- atom_bias_enc: bfloat16 [8192, 4, 128], P('tok'), may hold values from -8 to 248
- atom_bias_dec: bfloat16 [8192, 4, 128], P('tok'), may hold values from -8 to 248
- enc_project: bfloat16 [128, 384], replicated, may hold values from -0.5 to 0.5
- enc_mix: bfloat16 [128, 128], replicated, may hold values from -0.5 to 0.5
- pool_weight: bfloat16 [128, 768], replicated, may hold values from -0.5 to 0.5
- token_project: bfloat16 [768, 3072], replicated, may hold values from -0.21875 to 0.21875
- token_mix: bfloat16 [768, 768], replicated, may hold values from -0.21875 to 0.21875
- swiglu_in: bfloat16 [768, 3072], replicated, may hold values from -0.21875 to 0.21875
- swiglu_out: bfloat16 [1536, 768], replicated, may hold values from -0.15625 to 0.15625
- spread_weight: bfloat16 [768, 128], replicated, may hold values from -0.21875 to 0.21875
- dec_project: bfloat16 [128, 384], replicated, may hold values from -0.5 to 0.5
- dec_mix: bfloat16 [128, 128], replicated, may hold values from -0.5 to 0.5
Outputs:
- token_state: bfloat16 [1024, 8, 768], P('tok', 'seed')
- atom_update: bfloat16 [8192, 8, 128], P('tok', 'seed')
Inputs may be any that keep to these rules, and one draw needn't show every extreme that they name: `atom_index`: Nondecreasing. The atoms of token t are rows 8 t + e(t) to 8 (t + 1) + e(t + 1) - 1, every e between -3 and 3, e(0) = e(1024) = 0, and e(t) between -3 and -2 for every other t that is a multiple of 128; so every token has 2 to 14 atoms.
All inputs are finite; a program needn't handle non-finite values.
Results may differ from a plain program's by a relative error of at most 0.015.
Values may be sent and summed in bfloat16 or wider, within the bound.
A program may use at most 192 MiB of HBM per device.

v0:
```python
import jax
import jax.numpy as jnp
from jax import lax
from jax.sharding import PartitionSpec as P

HEADS = 16
QUERY_BLOCK = 32


EPS = 1e-05
NEGATIVE = -1000000000.0


def padded_2(block, sides, width):
    for axis, dim in sides:
        count = lax.axis_size(axis)
        forward = [(i, i + 1) for i in range(count - 1)]
        backward = [(target, source) for source, target in forward]
        low = lax.ppermute(
            lax.slice_in_dim(block, block.shape[dim] - width, None, axis=dim), axis, forward
        )
        high = lax.ppermute(lax.slice_in_dim(block, 0, width, axis=dim), axis, backward)
        block = jnp.concatenate([low, block, high], axis=dim)
    return block


def shifted(shard, axis, by):
    length = lax.axis_size(axis)
    pairs = [(i, i + by) for i in range(length) if 0 <= i + by < length]
    return lax.ppermute(shard, axis, pairs)


def layer_norm(values):
    centre = values - jnp.mean(values, axis=-1, keepdims=True)
    variance = jnp.mean(centre * centre, axis=-1, keepdims=True)
    return centre * lax.rsqrt(variance + EPS)


def atom_block(inputs, bias, project, mix):
    atom_rows, seed_count, atom_width = inputs.shape
    head_count = bias.shape[1]
    window_size = bias.shape[2]
    head_size = atom_width // head_count
    query_block = QUERY_BLOCK
    margin = (window_size - query_block) // 2
    block_count = atom_rows // query_block
    extra_tiles = window_size // query_block - 1
    normed = layer_norm(inputs.astype(jnp.float32)).astype(jnp.bfloat16)
    packed = jnp.dot(
        normed.reshape(atom_rows * seed_count, atom_width),
        project,
        preferred_element_type=jnp.float32,
    )
    packed = packed.astype(jnp.bfloat16).reshape(atom_rows, seed_count, 3 * atom_width)
    queries = packed[:, :, :atom_width].reshape(
        block_count, query_block, seed_count, head_count, head_size
    )
    padded = padded_2(packed[:, :, atom_width:], (("tok", 0),), margin)
    key_tiles = padded.reshape(block_count + extra_tiles, query_block, seed_count, 2 * atom_width)
    windows = jnp.concatenate(
        [key_tiles[offset : offset + block_count] for offset in range(extra_tiles + 1)], axis=1
    )
    key_rows = windows[..., :atom_width].reshape(
        block_count, window_size, seed_count, head_count, head_size
    )
    value_rows = windows[..., atom_width:].reshape(
        block_count, window_size, seed_count, head_count, head_size
    )
    scores = jnp.einsum(
        "bqshd,bkshd->bshqk", queries, key_rows, preferred_element_type=jnp.float32
    ) * head_size ** (-0.5)
    scores = (
        scores
        + bias.astype(jnp.float32)
        .reshape(block_count, query_block, head_count, window_size)
        .transpose(0, 2, 1, 3)[:, None]
    )
    first_atom = lax.axis_index("tok") * atom_rows
    position = (
        first_atom
        + query_block * jnp.arange(block_count, dtype=jnp.int32)[:, None]
        - margin
        + jnp.arange(window_size, dtype=jnp.int32)[None, :]
    )
    in_range = (position >= 0) & (position < atom_rows * lax.axis_size("tok"))
    scores = jnp.where(in_range[:, None, None, None, :], scores, NEGATIVE)
    row_max = jnp.max(scores, axis=-1, keepdims=True)
    weights = jnp.exp(scores - row_max)
    attended_atoms = jnp.einsum(
        "bshqk,bkshd->bqshd",
        weights.astype(jnp.bfloat16),
        value_rows,
        preferred_element_type=jnp.float32,
    )
    attended_atoms = attended_atoms / jnp.sum(weights, axis=-1).transpose(0, 3, 1, 2)[..., None]
    attended_atoms = attended_atoms.reshape(atom_rows * seed_count, atom_width).astype(jnp.bfloat16)
    update = jnp.dot(attended_atoms, mix, preferred_element_type=jnp.float32).reshape(
        atom_rows, seed_count, atom_width
    )
    return (inputs.astype(jnp.float32) + update).astype(jnp.bfloat16)


def token_attention(queries, key_rows, value_rows, bias):
    tok_rows, seed_count, head_count, head_size = queries.shape
    scale = head_size ** (-0.5)
    running_max = jnp.full((seed_count, head_count, tok_rows), NEGATIVE, jnp.float32)
    piece_keys = lax.all_gather(key_rows, "tok", axis=0, tiled=True)
    piece_values = lax.all_gather(value_rows, "tok", axis=0, tiled=True)
    bias_part = bias.astype(jnp.float32)
    scores = (
        jnp.einsum("qshd,kshd->shqk", queries, piece_keys, preferred_element_type=jnp.float32)
        * scale
        + bias_part[None]
    )
    new_max = jnp.maximum(running_max, jnp.max(scores, axis=-1))
    weights = jnp.exp(scores - new_max[..., None])
    running_sum = jnp.sum(weights, axis=-1)
    contribution = jnp.einsum(
        "shqk,kshd->shqd",
        weights.astype(jnp.bfloat16),
        piece_values,
        preferred_element_type=jnp.float32,
    )
    result = contribution / running_sum[..., None]
    return result.transpose(2, 0, 1, 3)


def per_device(
    atom_feats,
    atom_index,
    token_cond,
    pair_bias,
    atom_bias_enc,
    atom_bias_dec,
    enc_project,
    enc_mix,
    pool_weight,
    token_project,
    token_mix,
    swiglu_in,
    swiglu_out,
    spread_weight,
    dec_project,
    dec_mix,
):
    atom_rows, seed_count, atom_width = atom_feats.shape
    tok_rows, token_width = token_cond.shape
    head_count = HEADS
    head_size = token_width // head_count
    edge_rows = min(8, tok_rows)
    span_rows = tok_rows + edge_rows
    base_token = lax.axis_index("tok") * tok_rows
    encoded = atom_block(atom_feats, atom_bias_enc, enc_project, enc_mix)
    lifted = jnp.dot(
        encoded.reshape(atom_rows * seed_count, atom_width),
        pool_weight,
        preferred_element_type=jnp.float32,
    )
    lifted = (
        jnp.maximum(lifted, 0.0).astype(jnp.bfloat16).reshape(atom_rows, seed_count * token_width)
    )
    chosen = (
        atom_index[None, :] - base_token == jnp.arange(span_rows, dtype=jnp.int32)[:, None]
    ).astype(jnp.bfloat16)
    pool_terms = jnp.dot(chosen, lifted, preferred_element_type=jnp.float32)
    tallies = jnp.sum(chosen.astype(jnp.float32), axis=1)
    from_left = (
        shifted(pool_terms[tok_rows:].astype(jnp.bfloat16), "tok", 1).astype(jnp.float32),
        shifted(tallies[tok_rows:].astype(jnp.bfloat16), "tok", 1).astype(jnp.float32),
    )
    inner_rows = tok_rows - edge_rows
    pooled_sums = pool_terms[:tok_rows] + jnp.pad(from_left[0], ((0, inner_rows), (0, 0)))
    counts = tallies[:tok_rows] + jnp.pad(from_left[1], (0, inner_rows))
    residual = (
        token_cond.astype(jnp.float32)[:, None, :]
        + pooled_sums.reshape(tok_rows, seed_count, token_width) / counts[:, None, None]
    )
    normed = layer_norm(residual).astype(jnp.bfloat16).reshape(tok_rows * seed_count, token_width)
    projected = jnp.dot(normed, token_project, preferred_element_type=jnp.float32).reshape(
        tok_rows, seed_count, 4, head_count, head_size
    )
    queries = projected[:, :, 0].astype(jnp.bfloat16)
    key_rows = projected[:, :, 1].astype(jnp.bfloat16)
    value_rows = projected[:, :, 2].astype(jnp.bfloat16)
    gate_open = jax.nn.sigmoid(projected[:, :, 3])
    whole_bias = lax.all_gather(pair_bias, "seed", axis=0, tiled=True)
    attended = token_attention(queries, key_rows, value_rows, whole_bias)
    gated_out = (
        (attended * gate_open).astype(jnp.bfloat16).reshape(tok_rows * seed_count, token_width)
    )
    residual = residual + jnp.dot(gated_out, token_mix, preferred_element_type=jnp.float32).reshape(
        tok_rows, seed_count, token_width
    )
    normed = layer_norm(residual).astype(jnp.bfloat16).reshape(tok_rows * seed_count, token_width)
    widened = jnp.dot(normed, swiglu_in, preferred_element_type=jnp.float32)
    inner_width = swiglu_out.shape[0]
    hidden = (jax.nn.silu(widened[:, :inner_width]) * widened[:, inner_width:]).astype(jnp.bfloat16)
    lowered = jnp.dot(hidden, swiglu_out, preferred_element_type=jnp.float32).reshape(
        tok_rows, seed_count, token_width
    )
    token_state = (residual + lowered).astype(jnp.bfloat16)
    spread = jnp.dot(
        token_state.reshape(tok_rows * seed_count, token_width),
        spread_weight,
        preferred_element_type=jnp.float32,
    )
    spread = spread.astype(jnp.bfloat16).reshape(tok_rows, seed_count * atom_width)
    upper = shifted(spread[:edge_rows], "tok", -1)
    beside_all = jnp.concatenate([spread, upper], axis=0)
    picker = (
        atom_index[:, None] - base_token == jnp.arange(span_rows, dtype=jnp.int32)[None, :]
    ).astype(jnp.bfloat16)
    carried = jnp.dot(picker, beside_all, preferred_element_type=jnp.float32)
    decoded_in = (
        encoded.astype(jnp.float32) + carried.reshape(atom_rows, seed_count, atom_width)
    ).astype(jnp.bfloat16)
    atom_update = atom_block(decoded_in, atom_bias_dec, dec_project, dec_mix)
    return (token_state, atom_update)


def solution(mesh):
    placed = (
        P("tok", "seed", None),
        P("tok"),
        P("tok", None),
        P("seed", "tok", None),
        P("tok", None, None),
        P("tok", None, None),
        P(),
        P(),
        P(),
        P(),
        P(),
        P(),
        P(),
        P(),
        P(),
        P(),
    )
    return jax.shard_map(
        per_device,
        mesh=mesh,
        in_specs=placed,
        out_specs=(P("tok", "seed", None), P("tok", "seed", None)),
        check_vma=False,
    )
```

profile of v0, /device:TPU:1, one launch (start us, length us, event | category | flops | bytes accessed | tf_op | source)
XLA Modules:
  0.0 337.6 jit_solution(14501177121881152922)
XLA Ops:
  15.3 4.5 %reshape.235 = bf16[1024,2,384]{2,1,0:T(2,128)(2,1)} reshape(bf16[2048,384]{1,0:T(8,128)(2,1)} %convolution_convert_fusion.1) | data formatting | bytes 3145728 | tf_op jit(solution)/shard_map/reshape | solution.py:54
  20.8 4.6 %collective-permute-start = (bf16[48,2,256]{2,1,0:T(2,128)(2,1)S(1)}, bf16[48,2,256]{2,1,0:T(2,128)(2,1)}, u32[]{:S(2)}, u32[]{:S(2)}) collective-permute-start(bf16[48,2,256]{2,1,0:T(2,128)(2,1)S(1)} %get-tuple-element.22), channel_id=1, source_target_pairs={{0,1},{1,2},{2,3},{3,4},{4,5},{5,6},{6,7},{8,9},{9,10},{10,11},{11... | collective-permute-start | bytes 147464 | tf_op jit(solution)/shard_map/ppermute | solution.py:19
  27.5 3.6 %collective-permute-start.3 = (bf16[8]{0:T(256)(128)(2,1)S(1)}, bf16[8]{0:T(256)(128)(2,1)S(1)}, u32[]{:S(2)}, u32[]{:S(2)}) collective-permute-start(bf16[8]{0:T(256)(128)(2,1)S(1)} %slice.154), channel_id=1, source_target_pairs={{0,1},{1,2},{2,3},{3,4},{4,5},{5,6},{6,7},{8,9},{9,10},{10,11},{11... | collective-permute-start | bytes 56 | tf_op jit(solution)/shard_map/ppermute | solution.py:30
  33.6 2.9 copy.187
  38.4 6.9 %copy.124 = bf16[768,3072]{0,1:T(8,128)(2,1)} copy(bf16[768,3072]{1,0:T(8,128)(2,1)} %param.25) | data formatting | bytes 9437184 | tf_op args[9]
  45.3 13.9 %fusion.63 = (bf16[1024,2,256]{2,1,0:T(2,128)(2,1)}, bf16[1024,2,256]{2,1,0:T(2,128)(2,1)}, bf16[1024,2,256]{2,1,0:T(2,128)(2,1)}, bf16[1024,2,256]{2,1,0:T(2,128)(2,1)}) fusion(bf16[48,2,256]{2,1,0:T(2,128)(2,1)} %collective-permute-done, bf16[1024,2,256]{2,1,0:T(2,128)(2,1)S(1)} %slice-done, bf16[48,2,256]{2,1,0:T(2,128)(2,1)} %collective-permute-done.1), kind=kLoop, calls=%fused_computation.76 | loop fusion | flops 2097152 | bytes 5341184 | tf_op jit(solution)/shard_map/concatenate | solution.py:23
  59.2 5.7 %copy.110 = bf16[32,32,2,256]{1,3,2,0:T(8,128)(2,1)} copy(bf16[32,32,2,256]{3,2,1,0:T(2,128)(2,1)} %bitcast.144) | data formatting | bytes 2097152 | tf_op jit(solution)/shard_map/slice | solution.py:61
  64.9 5.7 %copy.111 = bf16[32,32,2,256]{1,3,2,0:T(8,128)(2,1)} copy(bf16[32,32,2,256]{3,2,1,0:T(2,128)(2,1)} %bitcast.142) | data formatting | bytes 2097152 | tf_op jit(solution)/shard_map/slice | solution.py:61
  70.6 5.6 %copy.112 = bf16[32,32,2,256]{1,3,2,0:T(8,128)(2,1)} copy(bf16[32,32,2,256]{3,2,1,0:T(2,128)(2,1)} %bitcast.140) | data formatting | bytes 2097152 | tf_op jit(solution)/shard_map/slice | solution.py:61
  76.2 4.9 %copy.113 = bf16[32,32,2,256]{1,3,2,0:T(8,128)(2,1)} copy(bf16[32,32,2,256]{3,2,1,0:T(2,128)(2,1)S(1)} %bitcast.138) | data formatting | bytes 2097152 | tf_op jit(solution)/shard_map/slice | solution.py:61
  81.2 8.8 %pad_maximum_fusion = bf16[32,128,2,256]{1,3,2,0:T(8,128)(2,1)S(1)} fusion(bf16[32,32,2,256]{1,3,2,0:T(8,128)(2,1)} %copy.113, bf16[32,32,2,256]{1,3,2,0:T(8,128)(2,1)} %copy.112, bf16[32,32,2,256]{1,3,2,0:T(8,128)(2,1)} %copy.111, bf16[32,32,2,256]{1,3,2,0:T(8,128)(2,1)} %copy.110), kind=kLoop, calls=%fused_computation.7 | loop fusion | flops 16777216 | bytes 8388608 | tf_op jit(solution)/shard_map/concatenate | solution.py:60
  101.0 3.7 %reshape.264 = bf16[1024,2,128]{0,2,1:T(8,128)(2,1)S(1)} reshape(bf16[32,32,2,4,32]{1,0,4,3,2:T(8,128)(2,1)} %copy.117) | data formatting | bytes 1048576 | tf_op jit(solution)/shard_map/convert_element_type | solution.py:96
  106.4 3.5 %maximum_convert_fusion = bf16[2048,768]{1,0:T(8,128)(2,1)} fusion(bf16[2048,128]{1,0:T(8,128)(2,1)S(1)} %bitcast.157, bf16[128,768]{1,0:T(8,128)(2,1)} %param.24), kind=kOutput, calls=%fused_computation.6 | convolution fusion | flops 405798912 | bytes 3866624 | tf_op jit(solution)/shard_map/dot_general | solution.py:154
  109.9 5.7 %reshape.241 = bf16[1024,1536]{1,0:T(8,128)(2,1)} reshape(bf16[2048,768]{1,0:T(8,128)(2,1)} %maximum_convert_fusion) | data formatting | bytes 6291456 | tf_op jit(solution)/shard_map/reshape | solution.py:160
  125.4 5.6 %fusion.105 = (bf16[128,2,4,16,48]{0,4,3,2,1:T(8,128)(2,1)S(1)}, f32[128,2,4,16,48]{0,4,3,2,1:T(8,128)}) fusion(bf16[4,16,48,768,1]{3,2,1,0,4:T(8,128)(2,1)} %bitcast.128, bf16[128,2,768,1,1]{2,1,0,4,3:T(2,128)(2,1)} %bitcast.159), kind=kOutput, calls=%fused_computation.147 | convolution fusion | flops 1208745984 | bytes 9830400 | tf_op jit(solution)/shard_map/dot_general | solution.py:179
  134.0 6.5 %convert_element_type.135 = f32[16,128,1024]{2,1,0:T(8,128)} convert(bf16[16,128,1024]{2,1,0:T(8,128)(2,1)} %all-gather.6.cloned.1.call-done) | non-fusion elementwise | flops 2097152 | bytes 12582912 | tf_op jit(solution)/shard_map/convert_element_type | solution.py:109
  140.4 34.0 %all-gather.8.cloned.1.call-done = bf16[1024,2,1,16,48]{0,4,3,2,1:T(8,128)(2,1)} async-done(((bf16[128,2,1,16,48]{0,4,3,2,1:T(8,128)(2,1)}), bf16[1024,2,1,16,48]{0,4,3,2,1:T(8,128)(2,1)}) %all-gather.8.cloned.1.call-update) | async-done | bytes 3145744 | tf_op jit(solution)/shard_map/all_gather | solution.py:107
  174.4 12.9 %fusion = (f32[2,16,128]{2,1,0:T(8,128)S(1)}, f32[2,16,128,1024]{3,2,1,0:T(8,128)}) fusion(f32[16,128,1024]{2,1,0:T(8,128)} %convert_element_type.135, bf16[1024,2,1,16,48]{0,4,3,2,1:T(8,128)(2,1)} %all-gather.8.cloned.1.call-done, bf16[128,2,4,16,48]{0,4,3,2,1:T(8,128)(2,1)} %copy-done.4), kind=kOutput, calls=%fused_computation.2 | convolution fusion | flops 415232000 | bytes 28721152 | tf_op jit(solution)/shard_map/qshd,kshd->shqk/dot_general | solution.py:111
  187.3 8.6 %fusion.1 = f32[2,16,128]{2,1,0:T(8,128)S(1)} fusion(f32[2,16,128,1024]{3,2,1,0:T(8,128)} %get-tuple-element.41, f32[2,16,128]{2,1,0:T(8,128)S(1)} %broadcast_maximum_fusion, f32[16,128,1024]{2,1,0:T(8,128)S(1)} %copy-done.1), kind=kLoop, calls=%fused_computation.3 | loop fusion | flops 16773120 | bytes 25198592 | tf_op jit(solution)/shard_map/reduce_sum | solution.py:117
  195.9 17.5 %all-gather.10.cloned.1.call-done = bf16[1024,2,1,16,48]{0,4,3,2,1:T(8,128)(2,1)} async-done(((bf16[128,2,1,16,48]{0,4,3,2,1:T(8,128)(2,1)}), bf16[1024,2,1,16,48]{0,4,3,2,1:T(8,128)(2,1)}) %all-gather.10.cloned.1.call-update) | async-done | bytes 3145744 | tf_op jit(solution)/shard_map/all_gather | solution.py:108
  213.5 11.4 %fusion.55 = bf16[128,2,16,48]{0,3,2,1:T(8,128)(2,1)S(1)} fusion(bf16[1024,2,1,16,48]{0,4,3,2,1:T(8,128)(2,1)} %all-gather.10.cloned.1.call-done, f32[2,16,128,1024]{3,2,1,0:T(8,128)} %get-tuple-element.41, f32[2,16,128]{2,1,0:T(8,128)S(1)} %broadcast_maximum_fusion, f32[16,128,1024]{2,1,0:T(8,128)} %convert_element_type.135, ...), kind=kOutput, calls=%fused_computation.63 | convolution fusion | flops 420610048 | bytes 29523968 | tf_op jit(solution)/shard_map/shqk,kshd->shqd/dot_general | solution.py:118
  227.2 3.9 %fusion.107 = f32[256,3072]{1,0:T(8,128)S(1)} fusion(bf16[256,768]{1,0:T(8,128)(2,1)} %reshape.243, bf16[768,3072]{1,0:T(8,128)(2,1)} %param.27), kind=kOutput, calls=%fused_computation.149 | convolution fusion | flops 1207959552 | bytes 8257536 | tf_op jit(solution)/shard_map/dot_general | solution.py:195
  253.5 4.5 %reshape.249 = bf16[1024,2,384]{2,1,0:T(2,128)(2,1)} reshape(bf16[2048,384]{1,0:T(8,128)(2,1)} %convolution_convert_fusion) | data formatting | bytes 3145728 | tf_op jit(solution)/shard_map/reshape | solution.py:54
  260.9 3.0 collective-permute-start.6
  266.8 2.9 slice.197
  271.7 11.6 %fusion.61 = (bf16[1024,2,256]{2,1,0:T(2,128)(2,1)}, bf16[1024,2,256]{2,1,0:T(2,128)(2,1)}, bf16[1024,2,256]{2,1,0:T(2,128)(2,1)}, bf16[1024,2,256]{2,1,0:T(2,128)(2,1)}) fusion(bf16[48,2,256]{2,1,0:T(2,128)(2,1)} %collective-permute-done.5, bf16[1024,2,256]{2,1,0:T(2,128)(2,1)} %slice.197, bf16[48,2,256]{2,1,0:T(2,128)(2,1)} %collective-permute-done.6), kind=kLoop, calls=%fused_computation.74 | loop fusion | flops 2097152 | bytes 5341184 | tf_op jit(solution)/shard_map/concatenate | solution.py:23
  283.3 5.6 %copy.132 = bf16[32,32,2,256]{1,3,2,0:T(8,128)(2,1)} copy(bf16[32,32,2,256]{3,2,1,0:T(2,128)(2,1)} %bitcast.145) | data formatting | bytes 2097152 | tf_op jit(solution)/shard_map/slice | solution.py:61
  288.9 5.7 %copy.133 = bf16[32,32,2,256]{1,3,2,0:T(8,128)(2,1)} copy(bf16[32,32,2,256]{3,2,1,0:T(2,128)(2,1)} %bitcast.143) | data formatting | bytes 2097152 | tf_op jit(solution)/shard_map/slice | solution.py:61
  294.6 5.6 %copy.134 = bf16[32,32,2,256]{1,3,2,0:T(8,128)(2,1)} copy(bf16[32,32,2,256]{3,2,1,0:T(2,128)(2,1)} %bitcast.141) | data formatting | bytes 2097152 | tf_op jit(solution)/shard_map/slice | solution.py:61
  300.2 5.6 %copy.135 = bf16[32,32,2,256]{1,3,2,0:T(8,128)(2,1)} copy(bf16[32,32,2,256]{3,2,1,0:T(2,128)(2,1)} %bitcast.139) | data formatting | bytes 2097152 | tf_op jit(solution)/shard_map/slice | solution.py:61
  305.9 8.8 %pad_maximum_fusion.1 = bf16[32,128,2,256]{1,3,2,0:T(8,128)(2,1)S(1)} fusion(bf16[32,32,2,256]{1,3,2,0:T(8,128)(2,1)} %copy.135, bf16[32,32,2,256]{1,3,2,0:T(8,128)(2,1)} %copy.134, bf16[32,32,2,256]{1,3,2,0:T(8,128)(2,1)} %copy.133, bf16[32,32,2,256]{1,3,2,0:T(8,128)(2,1)} %copy.132), kind=kLoop, calls=%fused_computation.8 | loop fusion | flops 16777216 | bytes 8388608 | tf_op jit(solution)/shard_map/concatenate | solution.py:60
  325.7 3.5 %reshape.266 = bf16[1024,2,128]{0,2,1:T(8,128)(2,1)S(1)} reshape(bf16[32,32,2,4,32]{1,0,4,3,2:T(8,128)(2,1)} %copy.139) | data formatting | bytes 1048576 | tf_op jit(solution)/shard_map/convert_element_type | solution.py:96
  (150 shorter events, 85.7 us)
Async XLA Ops:
  7.2 223.9 %copy-start = (bf16[1536,768]{1,0:T(8,128)(2,1)S(1)}, bf16[1536,768]{1,0:T(8,128)(2,1)}, u32[]{:S(2)}) copy-start(bf16[1536,768]{1,0:T(8,128)(2,1)} %param.28) | copy-start | bytes 7077892
  7.2 126.8 %all-gather.6.cloned.1.call-start = ((), (), s32[]{:S(2)}) async-start(), calls=%async_computation | async-start | bytes 5242880 | tf_op jit(solution)/shard_map/all_gather | solution.py:186
  8.8 18.6 %copy-start.23 = (s32[1024]{0:T(1024)S(1)}, s32[1024]{0:T(1024)}, u32[]{:S(2)}) copy-start(s32[1024]{0:T(1024)} %param.17) | copy-start | bytes 12292
  19.8 11.9 %slice-start.1 = ((bf16[1024,2,384]{2,1,0:T(2,128)(2,1)}), bf16[1024,2,128]{2,1,0:T(2,128)(2,1)S(1)}, s32[]{:S(2)}) async-start(bf16[1024,2,384]{2,1,0:T(2,128)(2,1)} %reshape.235), calls=%async_computation.4 | async-start | bytes 1048576 | tf_op jit(solution)/shard_map/slice | solution.py:55
  20.8 24.5 %collective-permute-start = (bf16[48,2,256]{2,1,0:T(2,128)(2,1)S(1)}, bf16[48,2,256]{2,1,0:T(2,128)(2,1)}, u32[]{:S(2)}, u32[]{:S(2)}) collective-permute-start(bf16[48,2,256]{2,1,0:T(2,128)(2,1)S(1)} %get-tuple-element.22), channel_id=1, source_target_pairs={{0,1},{1,2},{2,3},{3,4},{4,5},{5,6},{6,7},{8,9},{9,10},{10,11},{11... | collective-permute-start | bytes 147464 | tf_op jit(solution)/shard_map/ppermute | solution.py:19
  25.4 19.9 %collective-permute-start.1 = (bf16[48,2,256]{2,1,0:T(2,128)(2,1)S(1)}, bf16[48,2,256]{2,1,0:T(2,128)(2,1)}, u32[]{:S(2)}, u32[]{:S(2)}) collective-permute-start(bf16[48,2,256]{2,1,0:T(2,128)(2,1)S(1)} %get-tuple-element.23), channel_id=1, source_target_pairs={{1,0},{2,1},{3,2},{4,3},{5,4},{6,5},{7,6},{9,8},{10,9},{11,10},{12... | collective-permute-start | bytes 147464 | tf_op jit(solution)/shard_map/ppermute | solution.py:22
  27.5 92.6 %collective-permute-start.3 = (bf16[8]{0:T(256)(128)(2,1)S(1)}, bf16[8]{0:T(256)(128)(2,1)S(1)}, u32[]{:S(2)}, u32[]{:S(2)}) collective-permute-start(bf16[8]{0:T(256)(128)(2,1)S(1)} %slice.154), channel_id=1, source_target_pairs={{0,1},{1,2},{2,3},{3,4},{4,5},{5,6},{6,7},{8,9},{9,10},{10,11},{11... | collective-permute-start | bytes 56 | tf_op jit(solution)/shard_map/ppermute | solution.py:30
  31.2 143.3 %all-gather.8.cloned.1.call-start = ((), (), s32[]{:S(2)}) async-start(), calls=%async_computation.1 | async-start | bytes 3538944 | tf_op jit(solution)/shard_map/all_gather | solution.py:107
  31.8 4.7 %copy-start.19 = (bf16[128,768]{1,0:T(8,128)(2,1)S(1)}, bf16[128,768]{1,0:T(8,128)(2,1)}, u32[]{:S(2)}) copy-start(bf16[128,768]{1,0:T(8,128)(2,1)} %param.18) | copy-start | bytes 589828
  38.4 6.9 %slice-start = ((bf16[1024,2,384]{2,1,0:T(2,128)(2,1)}), bf16[1024,2,256]{2,1,0:T(2,128)(2,1)S(1)}, s32[]{:S(2)}) async-start(bf16[1024,2,384]{2,1,0:T(2,128)(2,1)} %reshape.235), calls=%async_computation.3 | async-start | bytes 2097152 | tf_op jit(solution)/shard_map/slice | solution.py:58
  64.9 11.4 %copy-start.14 = (bf16[1024,2,256]{2,1,0:T(2,128)(2,1)S(1)}, bf16[1024,2,256]{2,1,0:T(2,128)(2,1)}, u32[]{:S(2)}) copy-start(bf16[1024,2,256]{2,1,0:T(2,128)(2,1)} %get-tuple-element.34) | copy-start | bytes 3145732
  90.0 1.6 copy-start.3
  90.0 2.2 copy-start.5
  98.3 6.4 %copy-start.7 = (bf16[1024,2,128]{2,1,0:T(2,128)(2,1)S(1)}, bf16[1024,2,128]{2,1,0:T(2,128)(2,1)}, u32[]{:S(2)}) copy-start(bf16[1024,2,128]{2,1,0:T(2,128)(2,1)} %param.16) | copy-start | bytes 1572868
  98.3 6.4 %copy-start.21 = (bf16[128,128]{1,0:T(8,128)(2,1)S(1)}, bf16[128,128]{1,0:T(8,128)(2,1)}, u32[]{:S(2)}) copy-start(bf16[128,128]{1,0:T(8,128)(2,1)} %param.23) | copy-start | bytes 98308
  115.6 6.6 %copy-start.17 = (f32[128,768]{1,0:T(8,128)S(1)}, f32[128,768]{1,0:T(8,128)}, u32[]{:S(2)}) copy-start(f32[128,768]{1,0:T(8,128)} %convert_element_type.120) | copy-start | bytes 1179652
  118.2 3.1 collective-permute-start.2
  122.4 2.2 copy-start.8
  133.2 80.3 %all-gather.10.cloned.1.call-start = ((), (), s32[]{:S(2)}) async-start(), calls=%async_computation.2 | async-start | bytes 3538944 | tf_op jit(solution)/shard_map/all_gather | solution.py:108
  174.4 12.9 %copy-start.1 = (f32[16,128,1024]{2,1,0:T(8,128)S(1)}, f32[16,128,1024]{2,1,0:T(8,128)}, u32[]{:S(2)}) copy-start(f32[16,128,1024]{2,1,0:T(8,128)} %convert_element_type.135) | copy-start | bytes 25165828
  213.5 11.4 %copy-start.9 = (f32[128,2,768]{2,0,1:T(8,128)S(1)}, f32[128,2,768]{2,0,1:T(8,128)}, u32[]{:S(2)}) copy-start(f32[128,2,768]{2,0,1:T(8,128)} %copy-done.8) | copy-start | bytes 2359300
  213.5 11.4 %copy-start.18 = (bf16[768,768]{1,0:T(8,128)(2,1)S(1)}, bf16[768,768]{1,0:T(8,128)(2,1)}, u32[]{:S(2)}) copy-start(bf16[768,768]{1,0:T(8,128)(2,1)} %param.26) | copy-start | bytes 3538948
  236.8 11.6 %copy-start.13 = (bf16[1024,2,128]{2,0,1:T(8,128)(2,1)S(1)}, bf16[1024,2,128]{2,0,1:T(8,128)(2,1)}, u32[]{:S(2)}) copy-start(bf16[1024,2,128]{2,0,1:T(8,128)(2,1)} %copy-done.12) | copy-start | bytes 1572868
  237.2 8.6 %copy-start.16 = (bf16[128,2,768]{2,1,0:T(2,128)(2,1)}, bf16[128,2,768]{2,1,0:T(2,128)(2,1)S(1)}, u32[]{:S(2)}) copy-start(bf16[128,2,768]{2,1,0:T(2,128)(2,1)S(1)} %copy.141) | copy-start | bytes 1179652
  239.4 12.4 %copy-start.20 = (bf16[128,384]{1,0:T(8,128)(2,1)S(1)}, bf16[128,384]{1,0:T(8,128)(2,1)}, u32[]{:S(2)}) copy-start(bf16[128,384]{1,0:T(8,128)(2,1)} %param.30) | copy-start | bytes 294916
  239.4 4.9 %collective-permute-start.4 = (bf16[8,256]{1,0:T(8,128)(2,1)S(1)}, bf16[8,256]{1,0:T(8,128)(2,1)S(1)}, u32[]{:S(2)}, u32[]{:S(2)}) collective-permute-start(bf16[8,256]{1,0:T(8,128)(2,1)S(1)} %slice.162), channel_id=1, source_target_pairs={{1,0},{2,1},{3,2},{4,3},{5,4},{6,5},{7,6},{9,8},{10,9},{11,10},{12... | collective-permute-start | bytes 12296 | tf_op jit(solution)/shard_map/ppermute | solution.py:30
  258.0 11.6 %slice-start.2 = ((bf16[1024,2,384]{2,1,0:T(2,128)(2,1)}), bf16[1024,2,128]{2,1,0:T(2,128)(2,1)S(1)}, s32[]{:S(2)}) async-start(bf16[1024,2,384]{2,1,0:T(2,128)(2,1)} %reshape.249), calls=%async_computation.5 | async-start | bytes 1048576 | tf_op jit(solution)/shard_map/slice | solution.py:55
  259.0 12.7 %collective-permute-start.5 = (bf16[48,2,256]{2,1,0:T(2,128)(2,1)S(1)}, bf16[48,2,256]{2,1,0:T(2,128)(2,1)}, u32[]{:S(2)}, u32[]{:S(2)}) collective-permute-start(bf16[48,2,256]{2,1,0:T(2,128)(2,1)S(1)} %get-tuple-element.18), channel_id=1, source_target_pairs={{0,1},{1,2},{2,3},{3,4},{4,5},{5,6},{6,7},{8,9},{9,10},{10,11},{11... | collective-permute-start | bytes 147464 | tf_op jit(solution)/shard_map/ppermute | solution.py:19
  260.9 10.7 %collective-permute-start.6 = (bf16[48,2,256]{2,1,0:T(2,128)(2,1)S(1)}, bf16[48,2,256]{2,1,0:T(2,128)(2,1)}, u32[]{:S(2)}, u32[]{:S(2)}) collective-permute-start(bf16[48,2,256]{2,1,0:T(2,128)(2,1)S(1)} %get-tuple-element.19), channel_id=1, source_target_pairs={{1,0},{2,1},{3,2},{4,3},{5,4},{6,5},{7,6},{9,8},{10,9},{11,10},{12... | collective-permute-start | bytes 147464 | tf_op jit(solution)/shard_map/ppermute | solution.py:22
  314.7 1.6 copy-start.2
  314.7 2.2 copy-start.6
  323.0 6.2 %copy-start.22 = (bf16[128,128]{1,0:T(8,128)(2,1)S(1)}, bf16[128,128]{1,0:T(8,128)(2,1)}, u32[]{:S(2)}) copy-start(bf16[128,128]{1,0:T(8,128)(2,1)} %param.31) | copy-start | bytes 98308
  (5 other events, 5.4 us)
Sparse Core Ops, SparseCore 0:
  31.3 52.4 all-gather.5
  133.3 41.0 all-gather.7
  176.0 37.4 all-gather.9
where the time goes:
time: 343 us; the launch traced here: 338 us
  local copies, waits for them, and re-layouts  116 us (34%)
  other arithmetic  74.7 us (22%)
  matrix products  56.9 us (17%)
  waiting for transfers between devices  56.1 us (16%)
  starting transfers between devices  19.8 us (6%)
  between operations  14.6 us (4%)
    slice x8, local copies, waits for them, and re-layouts, atom_block(): key_tiles[offset:offset + block_count]  44.5 us
    all_gather x1, waiting for transfers between devices, token_attention(): piece_keys = lax.all_gather(key_rows, 'tok', axis=0, tiled=True)  34 us
    concatenate x2, other arithmetic, padded_2(): block = jnp.concatenate([low, block, high], axis=dim)  25.5 us
    concatenate x2, other arithmetic, atom_block(): jnp.concatenate([key_tiles[offset:offset + block_count] for offset in ran...  17.6 us
    all_gather x1, waiting for transfers between devices, token_attention(): piece_values = lax.all_gather(value_rows, 'tok', axis=0, tiled=True)  17.5 us
    unnamed x55, local copies, waits for them, and re-layouts  17.2 us
    dot_general x1, matrix products, token_attention(): jnp.einsum('qshd,kshd->shqk', queries, piece_keys, preferred_element_type...  12.9 us
    convert_element_type x4, local copies, waits for them, and re-layouts, atom_block(): attended_atoms.reshape(atom_rows * seed_count, atom_width)  12.6 us
  transfers between devices with their start and end apart: 10, of which 4 were waited for; matrix products, arithmetic and copies ran while one was open for 38% of the time, Pallas kernels for 0%

commit v1 on v0

v1 whole, which is shorter than its diff:
```python
import functools

import jax
import jax.numpy as jnp
from jax import lax
from jax.experimental import pallas as pl
from jax.experimental.pallas import tpu as pltpu
from jax.sharding import PartitionSpec as P

HEADS = 16
QUERY_BLOCK = 32
EPS = 1e-05
NEGATIVE = -1000000000.0
HALO = 128
RIM = 64
EDGE = 8
MISSING = -1000
BF = jnp.bfloat16
F32 = jnp.float32


def layer_norm(values):
    centre = values - jnp.mean(values, axis=-1, keepdims=True)
    variance = jnp.mean(centre * centre, axis=-1, keepdims=True)
    return centre * lax.rsqrt(variance + EPS)


def mm(a, b):
    return jnp.dot(a, b, preferred_element_type=F32)


def mm_t(a, b):
    return lax.dot_general(a, b, (((1,), (1,)), ((), ())), preferred_element_type=F32)


def iota(shape, dim):
    return lax.broadcasted_iota(jnp.int32, shape, dim)


def window_attention(packed, bias, mixed, blocks, key_base, low, high, group):
    seeds, _, triple = packed.shape
    width = triple // 3
    window = bias.shape[1]
    heads = bias.shape[0] // mixed.shape[1]
    size = width // heads
    rows = QUERY_BLOCK * heads
    margin = (window - QUERY_BLOCK) // 2
    repeat = (iota((rows, QUERY_BLOCK), 0) // heads == iota((rows, QUERY_BLOCK), 1)).astype(BF)
    join = (iota((QUERY_BLOCK, rows), 1) // heads == iota((QUERY_BLOCK, rows), 0)).astype(BF)
    own = (iota((rows, width), 0) % heads) == (iota((rows, width), 1) // size)
    lane = iota((rows, window), 1)

    def step(i, carry):
        for g in range(group):
            j = i * group + g
            start = pl.multiple_of(key_base + QUERY_BLOCK * j, 16)
            first = pl.multiple_of(QUERY_BLOCK * j, QUERY_BLOCK)
            term = bias[pl.ds(pl.multiple_of(rows * j, rows), rows), :].astype(F32)
            spot = lane + start
            valid = (spot >= low) & (spot < high)
            for s in range(seeds):
                query = packed[s, pl.ds(pl.multiple_of(start + margin, 16), QUERY_BLOCK), :width]
                query = jnp.where(own, mm(repeat, query), 0.0).astype(BF)
                keys = packed[s, pl.ds(start, window), width : 2 * width]
                values = packed[s, pl.ds(start, window), 2 * width :]
                scores = mm_t(query, keys) * size ** (-0.5) + term
                scores = jnp.where(valid, scores, NEGATIVE)
                weights = jnp.exp(scores - jnp.max(scores, axis=-1, keepdims=True))
                total = jnp.sum(weights, axis=-1, keepdims=True)
                part = mm(weights.astype(BF), values) / total
                part = jnp.where(own, part, 0.0).astype(BF)
                mixed[s, pl.ds(first, QUERY_BLOCK), :] = mm(join, part).astype(BF)
        return carry

    lax.fori_loop(0, blocks // group, step, 0)


def limits(tok, count, front, inner, total):
    low = jnp.where(tok == 0, front, 0)
    high = jnp.where(tok == count - 1, front + inner, total)
    return low, high


def encode_kernel(count, x, bias, index, cond, project, mix, pool, enc, residual, normed, packed, mixed):
    seeds, total, width = x.shape
    rows = mixed.shape[1]
    inner = rows - 2 * RIM
    low, high = limits(lax.axis_index("tok"), count, HALO, inner, total)
    for s in range(seeds):
        for at in range(0, total, 256):
            part = layer_norm(x[s, at : at + 256, :].astype(F32)).astype(BF)
            packed[s, at : at + 256, :] = mm(part, project[...]).astype(BF)
    window_attention(packed, bias, mixed, rows // QUERY_BLOCK, HALO - RIM - 48, low, high, 4)
    tokens = cond.shape[0]
    chosen = index[...] == iota((tokens, rows), 0)
    counts = jnp.sum(chosen.astype(F32), axis=1, keepdims=True)
    chosen = chosen.astype(BF)
    chunk = rows // 3
    for s in range(seeds):
        sums = jnp.zeros(residual.shape[1:], F32)
        for at in range(0, rows, chunk):
            base = x[s, at + HALO - RIM : at + HALO - RIM + chunk, :].astype(F32)
            part = (base + mm(mixed[s, at : at + chunk, :], mix[...])).astype(BF)
            enc[s, at : at + chunk, :] = part
            lifted = jnp.maximum(mm(part, pool[...]), 0.0).astype(BF)
            sums = sums + mm(chosen[:, at : at + chunk], lifted)
        state = cond[...].astype(F32) + sums / counts
        residual[s] = state
        normed[s] = layer_norm(state).astype(BF)


def token_kernel(
    own, everyone, bias_hbm, residual, project, mix_hbm, wide_hbm, down_hbm, spread_w,
    state_out, spread_out,
    kv, query, gate, attended, bias, mix, wide, down, sems,
):
    count, seeds, tokens, width = everyone.shape
    heads = bias.shape[0]
    size = width // heads
    copies = [
        pltpu.make_async_copy(source, target, sems.at[i])
        for i, (source, target) in enumerate(
            ((bias_hbm, bias), (mix_hbm, mix), (wide_hbm, wide), (down_hbm, down))
        )
    ]
    for copy in copies:
        copy.start()
    flat = own[...].reshape(seeds * tokens, width)
    query[...] = mm(flat, project[:, :width]).astype(BF).reshape(seeds, tokens, width)
    gate[...] = jax.nn.sigmoid(mm(flat, project[:, 3 * width :]))
    for s in range(seeds):
        for c in range(0, count, 2):
            part = everyone[c : c + 2, s].reshape(2 * tokens, width)
            for at in range(0, 2 * width, width):
                kv[s, c * tokens : (c + 2) * tokens, at : at + width] = mm(
                    part, project[:, width + at : 2 * width + at]
                ).astype(BF)
    copies[0].wait()
    span = 384
    group = span // size

    def step(i, carry):
        s = i // (heads // group)
        g = i % (heads // group)
        left = pl.multiple_of(g * span, 128)
        tiles = [jnp.zeros((tokens, 128), F32) for _ in range(span // 128)]
        for h in range(group):
            first = size * h // 128
            last = (size * h + size - 1) // 128
            wide_here = (last - first + 1) * 128
            lanes = pl.ds(left + first * 128, wide_here)
            spot = iota((tokens, wide_here), 1) + first * 128
            mine = (spot >= size * h) & (spot < size * (h + 1))
            q = query[s, :, lanes]
            q = jnp.where(mine, q, jnp.zeros_like(q))
            keys = kv[s, :, lanes]
            values = kv[s, :, pl.ds(left + width + first * 128, wide_here)]
            scores = mm_t(q, keys) * size ** (-0.5) + bias[g * group + h].astype(F32)
            weights = jnp.exp(scores - jnp.max(scores, axis=-1, keepdims=True))
            sums = jnp.sum(weights, axis=-1, keepdims=True)
            part = jnp.where(mine, mm(weights.astype(BF), values) / sums, 0.0)
            for t in range(first, last + 1):
                tiles[t] = tiles[t] + part[:, (t - first) * 128 : (t - first + 1) * 128]
        for t, tile in enumerate(tiles):
            attended[s, :, pl.ds(left + t * 128, 128)] = tile
        return carry

    lax.fori_loop(0, seeds * (heads // group), step, 0)
    copies[1].wait()
    gated = (attended[...].reshape(seeds * tokens, width) * gate[...]).astype(BF)
    state = residual[...].reshape(seeds * tokens, width) + mm(gated, mix[...])
    part = layer_norm(state).astype(BF)
    copies[2].wait()
    inner = down.shape[0]
    hidden = (jax.nn.silu(mm(part, wide[:, :inner])) * mm(part, wide[:, inner:])).astype(BF)
    copies[3].wait()
    state = (state + mm(hidden, down[...])).astype(BF)
    state_out[...] = state.reshape(seeds, tokens, width)
    spread_out[...] = mm(state, spread_w[...]).astype(BF).reshape(spread_out.shape)


def decode_kernel(count, enc, spread, index, bias, project, mix, out, decoded, packed, mixed):
    seeds, rows, width = enc.shape
    inner = out.shape[1]
    low, high = limits(lax.axis_index("tok"), count, RIM, inner, rows)
    picker = (index[...] == iota((spread.shape[1], rows), 0) - EDGE).astype(BF)
    chunk = rows // 3
    for s in range(seeds):
        for at in range(0, rows, chunk):
            carried = lax.dot_general(
                picker[:, at : at + chunk], spread[s], (((0,), (0,)), ((), ())),
                preferred_element_type=F32,
            )
            part = (enc[s, at : at + chunk, :].astype(F32) + carried).astype(BF)
            decoded[s, at : at + chunk, :] = part
            part = layer_norm(part.astype(F32)).astype(BF)
            packed[s, at : at + chunk, :] = mm(part, project[...]).astype(BF)
    window_attention(packed, bias, mixed, inner // QUERY_BLOCK, RIM - 48, low, high, 4)
    for s in range(seeds):
        for at in range(0, inner, 256):
            base = decoded[s, RIM + at : RIM + at + 256, :].astype(F32)
            out[s, at : at + 256, :] = (base + mm(mixed[s, at : at + 256, :], mix[...])).astype(BF)


PARAMS = pltpu.CompilerParams(vmem_limit_bytes=50 * 1024 * 1024)


def exchange(to_above, to_below):
    count = lax.axis_size("tok")
    above = [(i, i + 1) for i in range(count - 1)]
    below = [(target, source) for source, target in above]
    return lax.ppermute(to_above, "tok", above), lax.ppermute(to_below, "tok", below)


def per_device(
    atom_feats, atom_index, token_cond, pair_bias, atom_bias_enc, atom_bias_dec,
    enc_project, enc_mix, pool_weight, token_project, token_mix, swiglu_in, swiglu_out,
    spread_weight, dec_project, dec_mix,
):
    atoms, seeds, width = atom_feats.shape
    tokens, token_width = token_cond.shape
    atom_heads, window = atom_bias_enc.shape[1:]
    count = lax.axis_size("tok")
    tok = lax.axis_index("tok")
    whole_bias = lax.all_gather(pair_bias, "seed", axis=0, tiled=True)

    relative = atom_index - tok * tokens
    x = atom_feats.transpose(1, 0, 2)
    enc_bias = atom_bias_enc.reshape(atoms * atom_heads, window)
    dec_bias = atom_bias_dec.reshape(atoms * atom_heads, window)

    def parcel(at, at_rim):
        row = jnp.zeros((8, width), BF).at[0, :RIM].set(relative[at_rim : at_rim + RIM].astype(BF))
        rim = atom_heads * at_rim
        return jnp.concatenate(
            [
                x[:, at : at + HALO].reshape(seeds * HALO, width),
                enc_bias[rim : rim + atom_heads * RIM],
                row,
            ]
        )

    def unpack(parcel):
        cut = seeds * HALO
        end = cut + atom_heads * RIM
        return (
            parcel[:cut].reshape(seeds, HALO, width),
            parcel[cut:end],
            parcel[end, :RIM].astype(jnp.int32),
        )

    lower, upper = exchange(parcel(atoms - HALO, atoms - RIM), parcel(0, 0))
    lower_x, lower_bias, lower_index = unpack(lower)
    upper_x, upper_bias, upper_index = unpack(upper)
    x_ext = jnp.concatenate([lower_x, x, upper_x], axis=1)
    bias_ext = jnp.concatenate([lower_bias, enc_bias, upper_bias])
    lower_index = jnp.where(tok == 0, MISSING, lower_index - tokens)
    upper_index = jnp.where(tok == count - 1, MISSING, upper_index + tokens)
    index_ext = jnp.concatenate([lower_index, relative, upper_index])[None]
    rows = atoms + 2 * RIM

    encoded, residual, normed = pl.pallas_call(
        functools.partial(encode_kernel, count),
        out_shape=(
            jax.ShapeDtypeStruct((seeds, rows, width), BF),
            jax.ShapeDtypeStruct((seeds, tokens, token_width), F32),
            jax.ShapeDtypeStruct((seeds, tokens, token_width), BF),
        ),
        scratch_shapes=[
            pltpu.VMEM((seeds, atoms + 2 * HALO, 3 * width), BF),
            pltpu.VMEM((seeds, rows, width), BF),
        ],
        compiler_params=PARAMS,
        name="encode",
    )(x_ext, bias_ext, index_ext, token_cond, enc_project, enc_mix, pool_weight)

    everyone = lax.all_gather(normed, "tok", axis=0)
    vmem = pl.BlockSpec(memory_space=pltpu.VMEM)
    hbm = pl.BlockSpec(memory_space=pl.ANY)
    all_tokens = count * tokens
    state, spread = pl.pallas_call(
        token_kernel,
        out_shape=(
            jax.ShapeDtypeStruct((seeds, tokens, token_width), BF),
            jax.ShapeDtypeStruct((seeds, tokens, width), BF),
        ),
        in_specs=[vmem, vmem, hbm, vmem, vmem, hbm, hbm, hbm, vmem],
        scratch_shapes=[
            pltpu.VMEM((seeds, all_tokens, 2 * token_width), BF),
            pltpu.VMEM((seeds, tokens, token_width), BF),
            pltpu.VMEM((seeds * tokens, token_width), F32),
            pltpu.VMEM((seeds, tokens, token_width), F32),
            pltpu.VMEM(whole_bias.shape, BF),
            pltpu.VMEM(token_mix.shape, BF),
            pltpu.VMEM(swiglu_in.shape, BF),
            pltpu.VMEM(swiglu_out.shape, BF),
            pltpu.SemaphoreType.DMA((4,)),
        ],
        compiler_params=PARAMS,
        name="token",
    )(normed, everyone, whole_bias, residual, token_project, token_mix, swiglu_in, swiglu_out,
      spread_weight)

    low_rows, high_rows = exchange(spread[:, tokens - EDGE :], spread[:, :EDGE])
    spread_ext = jnp.concatenate([low_rows, spread, high_rows], axis=1)
    update = pl.pallas_call(
        functools.partial(decode_kernel, count),
        out_shape=jax.ShapeDtypeStruct((seeds, atoms, width), BF),
        scratch_shapes=[
            pltpu.VMEM((seeds, rows, width), BF),
            pltpu.VMEM((seeds, rows, 3 * width), BF),
            pltpu.VMEM((seeds, atoms, width), BF),
        ],
        compiler_params=PARAMS,
        name="decode",
    )(encoded, spread_ext, index_ext, dec_bias, dec_project, dec_mix)
    return state.transpose(1, 0, 2), update.transpose(1, 0, 2)


def solution(mesh):
    placed = (
        P("tok", "seed", None),
        P("tok"),
        P("tok", None),
        P("seed", "tok", None),
        P("tok", None, None),
        P("tok", None, None),
    ) + (P(),) * 10
    return jax.shard_map(
        per_device,
        mesh=mesh,
        in_specs=placed,
        out_specs=(P("tok", "seed", None), P("tok", "seed", None)),
        check_vma=False,
    )
```

time: 343 us -> 228 us (0.66); the launches traced: 338 us -> 228 us
  local copies, waits for them, and re-layouts: 116 us -> 4.88 us
  Pallas kernels: 0 us -> 96.6 us
  other arithmetic: 74.7 us -> 1.91 us
  matrix products: 56.9 us -> 0 us
  waiting for transfers between devices: 56.1 us -> 97.4 us
  starting transfers between devices: 19.8 us -> 12.7 us
    pallas_call x0 -> x3, Pallas kernels: none -> 96.6 us  [the longest x1 39.5 us: per_device(): pl.pallas_call(functools.partial(encode_kernel, count), out_shape=(jax.Sh...]
    dot_general x18 -> x0, matrix products: 56.9 us -> none  [the longest x1 12.9 us: token_attention(): jnp.einsum('qshd,kshd->shqk', queries, piece_keys, preferred_element_type...]
    all_gather x1, waiting for transfers between devices: 0.02 us -> 53 us  [per_device(): whole_bias = lax.all_gather(pair_bias, 'seed', axis=0, tiled=True)]
    slice x24 -> x5, local copies, waits for them, and re-layouts: 50.9 us -> 0.95 us  [the longest x1 0.92 us: parcel(): enc_bias[rim:rim + atom_heads * RIM]]
    concatenate x4 -> x5, other arithmetic: 43.1 us -> 1.2 us  [the longest x1 1.13 us: per_device(): bias_ext = jnp.concatenate([lower_bias, enc_bias, upper_bias])]
    reshape x10 -> x0, local copies, waits for them, and re-layouts: 25.4 us -> none  [the longest x2 9.05 us: atom_block(): packed.astype(jnp.bfloat16).reshape(atom_rows, seed_count, 3 * atom_width)]
    reduce_sum x11 -> x0, other arithmetic: 20.2 us -> none  [the longest x1 8.61 us: token_attention(): running_sum = jnp.sum(weights, axis=-1)]
    convert_element_type x9 -> x0, local copies, waits for them, and re-layouts: 15.4 us -> none  [the longest x4 12.6 us: atom_block(): attended_atoms.reshape(atom_rows * seed_count, atom_width)]
  transfers between devices with their start and end apart: 10 -> 6, of which waited for: 4 -> 4; matrix products, arithmetic and copies ran while one was open for 38% -> 1% of each run, Pallas kernels for 0% -> 0%
where the time goes in v1:
time: 228 us
  waiting for transfers between devices  97.4 us (43%)
  Pallas kernels  96.6 us (42%)
  between operations  14.3 us (6%)
  starting transfers between devices  12.7 us (6%)
  local copies, waits for them, and re-layouts  4.88 us (2%)
    all_gather x1, waiting for transfers between devices, per_device(): whole_bias = lax.all_gather(pair_bias, 'seed', axis=0, tiled=True)  53 us
    pallas_call x1, Pallas kernels, per_device(): pl.pallas_call(functools.partial(encode_kernel, count), out_shape=(jax.Sh...  39.5 us
    all_gather x1, waiting for transfers between devices, per_device(): everyone = lax.all_gather(normed, 'tok', axis=0)  37.8 us
    pallas_call x1, Pallas kernels, per_device(): pl.pallas_call(functools.partial(decode_kernel, count), out_shape=jax.Sha...  32.7 us
    pallas_call x1, Pallas kernels, per_device(): pl.pallas_call(token_kernel, out_shape=(jax.ShapeDtypeStruct((seeds, toke...  24.3 us
    ppermute x2, starting transfers between devices, exchange(): lax.ppermute(to_above, 'tok', above)  8.39 us
    ppermute x2, waiting for transfers between devices, exchange(): lax.ppermute(to_below, 'tok', below)  5.97 us
  transfers between devices with their start and end apart: 6, of which 4 were waited for; matrix products, arithmetic and copies ran while one was open for 1% of the time, Pallas kernels for 0%

profile of v1, /device:TPU:1, one launch (start us, length us, event | category | flops | bytes accessed | tf_op | source)
XLA Modules:
  0.0 227.7 jit_solution(10074532583482639166)
XLA Ops:
  7.2 0.0 all-gather.6.cloned.1.call-start
  7.2 0.7 fusion.8
  7.9 0.1 slice_bitcast_fusion.1
  8.0 0.9 fusion.9
  8.9 1.1 copy.25
  10.0 0.0 copy-start.9
  10.1 4.7 %collective-permute-start = (bf16[520,128]{1,0:T(8,128)(2,1)S(1)}, bf16[520,128]{1,0:T(8,128)(2,1)S(1)}, u32[]{:S(2)}, u32[]{:S(2)}) collective-permute-start(bf16[520,128]{1,0:T(8,128)(2,1)S(1)} %fusion.2), channel_id=1, source_target_pairs={{0,1},{1,2},{2,3},{3,4},{4,5},{5,6},{6,7},{8,9},{9,10},{10,11},{11... | collective-permute-start | bytes 399368 | tf_op jit(solution)/shard_map/ppermute | solution.py:212
  14.8 1.9 collective-permute-start.1
  16.8 0.0 collective-permute-done
  16.8 4.3 %collective-permute-done.1 = bf16[520,128]{1,0:T(8,128)(2,1)S(1)} collective-permute-done((bf16[520,128]{1,0:T(8,128)(2,1)S(1)}, bf16[520,128]{1,0:T(8,128)(2,1)S(1)}, u32[]{:S(2)}, u32[]{:S(2)}) %collective-permute-start.1) | collective-permute-done | bytes 133152 | tf_op jit(solution)/shard_map/ppermute | solution.py:212
  21.1 0.1 concatenate.26
  21.3 0.0 copy-start.3
  21.3 0.0 copy-start.4
  21.3 0.0 copy-start.5
  21.4 0.0 copy-start.7
  21.4 1.1 pad_maximum_fusion.bias
  22.5 0.1 copy-done.5
  22.6 39.5 %encode.1 = (bf16[2,1152,128]{2,1,0:T(8,128)(2,1)S(1)}, f32[2,128,768]{2,1,0:T(8,128)S(1)}, bf16[2,128,768]{2,1,0:T(8,128)(2,1)}) custom-call(bf16[2,1280,128]{2,1,0:T(8,128)(2,1)S(1)} %pad_maximum_fusion.1.x, bf16[4608,128]{1,0:T(8,128)(2,1)} %pad_maximum_fusion.bias, s32[1,1152]{1,0:T(1,128)S(1)} %broadcast_in_dim.9.index, bf16[128,768]{1,0:T(8,128)(2,1)S(1)} %copy-done.3, ...), custom_call_target="tpu_custom_call" | custom-call | tf_op jit(solution)/shard_map/encode/pallas_call | solution.py:262
  62.2 0.0 all-gather.6.cloned.1.call-update
  62.2 0.2 all-gather.4.cloned.1.call-start
  62.4 0.5 all-gather.4.cloned.1.call-update
  62.9 37.8 %all-gather.6.cloned.1.call-done = bf16[16,128,768]{2,1,0:T(8,128)(2,1)} async-done(((bf16[2,128,768]{2,1,0:T(8,128)(2,1)}), bf16[16,128,768]{2,1,0:T(8,128)(2,1)}) %all-gather.6.cloned.1.call-update) | async-done | bytes 3145744 | tf_op jit(solution)/shard_map/all_gather | solution.py:277
  100.7 53.0 %all-gather.4.cloned.1.call-done.bias_hbm = bf16[16,128,1024]{2,1,0:T(8,128)(2,1)} async-done(((bf16[4,128,1024]{2,1,0:T(8,128)(2,1)}), bf16[16,128,1024]{2,1,0:T(8,128)(2,1)}) %all-gather.4.cloned.1.call-update) | async-done | bytes 4194320 | tf_op jit(solution)/shard_map/all_gather | solution.py:225
  153.8 0.0 copy-start.8
  153.8 24.3 %token_.1 = (bf16[2,128,768]{2,1,0:T(8,128)(2,1)S(1)}, bf16[2,128,128]{2,1,0:T(8,128)(2,1)S(1)}) custom-call(bf16[2,128,768]{2,1,0:T(8,128)(2,1)} %get-tuple-element.31.own, bf16[8,2,128,768]{3,2,1,0:T(8,128)(2,1)} %bitcast.25, bf16[16,128,1024]{2,1,0:T(8,128)(2,1)} %all-gather.4.cloned.1.call-done.bias_hbm, f32[2,128,768]{2,1,0:T(8,128)S(1)} %get-tuple-element.32.residual, ...), custom_call_target="tpu_custom_call" | custom-call | tf_op jit(solution)/shard_map/token/pallas_call | solution.py:281
  178.2 3.7 %collective-permute-start.2 = (bf16[2,8,128]{2,1,0:T(8,128)(2,1)S(1)}, bf16[2,8,128]{2,1,0:T(8,128)(2,1)S(1)}, u32[]{:S(2)}, u32[]{:S(2)}) collective-permute-start(bf16[2,8,128]{2,1,0:T(8,128)(2,1)S(1)} %get-tuple-element.50), channel_id=1, source_target_pairs={{0,1},{1,2},{2,3},{3,4},{4,5},{5,6},{6,7},{8,9},{9,10},{10,11},{11... | collective-permute-start | bytes 12296 | tf_op jit(solution)/shard_map/ppermute | solution.py:212
  181.8 2.1 collective-permute-start.3
  184.0 1.2 copy.22
  185.1 0.0 collective-permute-done.2
  185.1 1.6 collective-permute-done.3
  186.8 32.7 %decode.1 = bf16[2,1024,128]{2,1,0:T(8,128)(2,1)S(1)} custom-call(bf16[2,1152,128]{2,1,0:T(8,128)(2,1)S(1)} %get-tuple-element.34.enc, bf16[2,144,128]{2,1,0:T(8,128)(2,1)S(1)} %pad_maximum_fusion.2.spread, s32[1,1152]{1,0:T(1,128)S(1)} %broadcast_in_dim.9.index, bf16[4096,128]{1,0:T(8,128)(2,1)S(1)} %bitcast.23, bf16[128,384]{1,0:T(8,128)(2,1)S(1)} %copy-done.6, ...), custom_call_target="tpu_custom_call" | custom-call | tf_op jit(solution)/shard_map/decode/pallas_call | solution.py:306
  219.5 1.3 copy.23
  (24 shorter events, 0.2 us)
Async XLA Ops:
  7.2 93.6 %all-gather.6.cloned.1.call-start = ((), (), s32[]{:S(2)}) async-start(), calls=%async_computation.1 | async-start | bytes 3538944 | tf_op jit(solution)/shard_map/all_gather | solution.py:277
  10.0 11.3 %copy-start.9 = (bf16[1024,4,128]{2,1,0:T(4,128)(2,1)S(1)}, bf16[1024,4,128]{2,1,0:T(4,128)(2,1)}, u32[]{:S(2)}) copy-start(bf16[1024,4,128]{2,1,0:T(4,128)(2,1)} %param.24) | copy-start | bytes 3145732
  10.1 6.7 %collective-permute-start = (bf16[520,128]{1,0:T(8,128)(2,1)S(1)}, bf16[520,128]{1,0:T(8,128)(2,1)S(1)}, u32[]{:S(2)}, u32[]{:S(2)}) collective-permute-start(bf16[520,128]{1,0:T(8,128)(2,1)S(1)} %fusion.2), channel_id=1, source_target_pairs={{0,1},{1,2},{2,3},{3,4},{4,5},{5,6},{6,7},{8,9},{9,10},{10,11},{11... | collective-permute-start | bytes 399368 | tf_op jit(solution)/shard_map/ppermute | solution.py:212
  14.8 6.3 %collective-permute-start.1 = (bf16[520,128]{1,0:T(8,128)(2,1)S(1)}, bf16[520,128]{1,0:T(8,128)(2,1)S(1)}, u32[]{:S(2)}, u32[]{:S(2)}) collective-permute-start(bf16[520,128]{1,0:T(8,128)(2,1)S(1)} %fusion.3), channel_id=1, source_target_pairs={{1,0},{2,1},{3,2},{4,3},{5,4},{6,5},{7,6},{9,8},{10,9},{11,10},{12... | collective-permute-start | bytes 399368 | tf_op jit(solution)/shard_map/ppermute | solution.py:212
  21.3 1.2 copy-start.3
  21.3 1.2 copy-start.4
  21.3 1.3 copy-start.5
  21.4 1.3 copy-start.7
  62.2 91.6 %copy-start = (bf16[768,768]{1,0:T(8,128)(2,1)S(1)}, bf16[768,768]{1,0:T(8,128)(2,1)}, u32[]{:S(2)}) copy-start(bf16[768,768]{1,0:T(8,128)(2,1)} %mix_hbm.1) | copy-start | bytes 3538948
  62.2 91.6 %copy-start.2 = (bf16[768,128]{1,0:T(8,128)(2,1)S(1)}, bf16[768,128]{1,0:T(8,128)(2,1)}, u32[]{:S(2)}) copy-start(bf16[768,128]{1,0:T(8,128)(2,1)} %spread_w.1) | copy-start | bytes 589828
  62.2 91.6 %all-gather.4.cloned.1.call-start = ((), (), s32[]{:S(2)}) async-start(), calls=%async_computation | async-start | bytes 5242880 | tf_op jit(solution)/shard_map/all_gather | solution.py:225
  153.8 33.0 %copy-start.1 = (bf16[1024,4,128]{2,1,0:T(4,128)(2,1)S(1)}, bf16[1024,4,128]{2,1,0:T(4,128)(2,1)}, u32[]{:S(2)}) copy-start(bf16[1024,4,128]{2,1,0:T(4,128)(2,1)} %param.25) | copy-start | bytes 3145732
  153.8 33.0 %copy-start.6 = (bf16[128,384]{1,0:T(8,128)(2,1)S(1)}, bf16[128,384]{1,0:T(8,128)(2,1)}, u32[]{:S(2)}) copy-start(bf16[128,384]{1,0:T(8,128)(2,1)} %project.5) | copy-start | bytes 294916
  153.8 33.0 %copy-start.8 = (bf16[128,128]{1,0:T(8,128)(2,1)S(1)}, bf16[128,128]{1,0:T(8,128)(2,1)}, u32[]{:S(2)}) copy-start(bf16[128,128]{1,0:T(8,128)(2,1)} %mix.3) | copy-start | bytes 98308
  178.2 7.0 %collective-permute-start.2 = (bf16[2,8,128]{2,1,0:T(8,128)(2,1)S(1)}, bf16[2,8,128]{2,1,0:T(8,128)(2,1)S(1)}, u32[]{:S(2)}, u32[]{:S(2)}) collective-permute-start(bf16[2,8,128]{2,1,0:T(8,128)(2,1)S(1)} %get-tuple-element.50), channel_id=1, source_target_pairs={{0,1},{1,2},{2,3},{3,4},{4,5},{5,6},{6,7},{8,9},{9,10},{10,11},{11... | collective-permute-start | bytes 12296 | tf_op jit(solution)/shard_map/ppermute | solution.py:212
  181.8 4.9 %collective-permute-start.3 = (bf16[2,8,128]{2,1,0:T(8,128)(2,1)S(1)}, bf16[2,8,128]{2,1,0:T(8,128)(2,1)S(1)}, u32[]{:S(2)}, u32[]{:S(2)}) collective-permute-start(bf16[2,8,128]{2,1,0:T(8,128)(2,1)S(1)} %get-tuple-element.51), channel_id=1, source_target_pairs={{1,0},{2,1},{3,2},{4,3},{5,4},{6,5},{7,6},{9,8},{10,9},{11,10},{12... | collective-permute-start | bytes 12296 | tf_op jit(solution)/shard_map/ppermute | solution.py:212
Sparse Core Ops, SparseCore 0:
  62.3 38.3 all-gather.5
  102.6 51.1 all-gather.3

commit v2 on v1

v2 whole, which is shorter than its diff:
```python
import functools

import jax
import jax.numpy as jnp
from jax import lax
from jax.experimental import pallas as pl
from jax.experimental.pallas import tpu as pltpu
from jax.sharding import PartitionSpec as P

HEADS = 16
QUERY_BLOCK = 32
EPS = 1e-05
NEGATIVE = -1000000000.0
HALO = 128
RIM = 64
EDGE = 8
MISSING = -1000
BF = jnp.bfloat16
F32 = jnp.float32


def layer_norm(values):
    centre = values - jnp.mean(values, axis=-1, keepdims=True)
    variance = jnp.mean(centre * centre, axis=-1, keepdims=True)
    return centre * lax.rsqrt(variance + EPS)


def mm(a, b):
    return jnp.dot(a, b, preferred_element_type=F32)


def mm_t(a, b):
    return lax.dot_general(a, b, (((1,), (1,)), ((), ())), preferred_element_type=F32)


def iota(shape, dim):
    return lax.broadcasted_iota(jnp.int32, shape, dim)


def window_attention(packed, bias, mixed, blocks, key_base, low, high, group):
    seeds, _, quad = packed.shape
    width = quad // 4
    window = bias.shape[1]
    heads = bias.shape[0] // mixed.shape[1]
    size = width // heads
    rows = QUERY_BLOCK * heads
    margin = (window - QUERY_BLOCK) // 2
    column = iota((QUERY_BLOCK, width), 1) // size
    lane = iota((rows, window), 1)

    def step(i, carry):
        scores, places = [], []
        for g in range(group):
            j = i * group + g
            start = pl.multiple_of(key_base + QUERY_BLOCK * j, 16)
            term = bias[pl.ds(pl.multiple_of(rows * j, rows), rows), :].astype(F32)
            spot = lane + start
            term = jnp.where((spot >= low) & (spot < high), term, NEGATIVE)
            for s in range(seeds):
                query = packed[s, pl.ds(pl.multiple_of(start + margin, 16), QUERY_BLOCK), :width]
                query = jnp.concatenate(
                    [jnp.where(column == h, query, jnp.zeros_like(query)) for h in range(heads)]
                )
                keys = packed[s, pl.ds(start, window), width : 2 * width]
                scores.append(mm_t(query, keys) * size ** (-0.5) + term)
                places.append((s, j, start))
        weights = [
            jnp.exp(part - jnp.max(part, axis=-1, keepdims=True)).astype(BF) for part in scores
        ]
        sums = [
            mm(part, packed[s, pl.ds(start, window), 2 * width :])
            for part, (s, _, start) in zip(weights, places)
        ]
        for part, (s, j, _) in zip(sums, places):
            part = part[:, :width] / part[:, width:]
            total = part[:QUERY_BLOCK]
            for h in range(1, heads):
                total = jnp.where(column == h, part[QUERY_BLOCK * h : QUERY_BLOCK * (h + 1)], total)
            first = pl.multiple_of(QUERY_BLOCK * j, QUERY_BLOCK)
            mixed[s, pl.ds(first, QUERY_BLOCK), :] = total.astype(BF)
        return carry

    lax.fori_loop(0, blocks // group, step, 0)


def limits(tok, count, front, inner, total):
    low = jnp.where(tok == 0, front, 0)
    high = jnp.where(tok == count - 1, front + inner, total)
    return low, high


def encode(low, high, x, bias, index, cond, project, mix, pool, enc, residual, packed, mixed):
    seeds, total, width = x.shape
    rows = mixed.shape[1]
    for s in range(seeds):
        for at in range(0, total, 256):
            part = layer_norm(x[s, at : at + 256, :].astype(F32)).astype(BF)
            packed[s, at : at + 256, : 3 * width] = mm(part, project[...]).astype(BF)
    packed[:, :, 3 * width :] = jnp.ones((seeds, total, width), BF)
    window_attention(packed, bias, mixed, rows // QUERY_BLOCK, HALO - RIM - 48, low, high, 2)
    tokens = cond.shape[0]
    chosen = index[...] == iota((tokens, rows), 0)
    counts = jnp.sum(chosen.astype(F32), axis=1, keepdims=True)
    chosen = chosen.astype(BF)
    chunk = rows // 3
    for s in range(seeds):
        sums = jnp.zeros(residual.shape[1:], F32)
        for at in range(0, rows, chunk):
            base = x[s, at + HALO - RIM : at + HALO - RIM + chunk, :].astype(F32)
            part = (base + mm(mixed[s, at : at + chunk, :], mix[...])).astype(BF)
            enc[s, at : at + chunk, :] = part
            lifted = jnp.maximum(mm(part, pool[...]), 0.0).astype(BF)
            sums = sums + mm(chosen[:, at : at + chunk], lifted)
        residual[s] = cond[...].astype(F32) + sums / counts


def attend(bias, query, kv, attended):
    seeds, tokens, width = query.shape
    heads = bias.shape[0]
    size = width // heads
    span = 384
    group = span // size

    def step(i, carry):
        s = i // (heads // group)
        g = i % (heads // group)
        left = pl.multiple_of(g * span, 128)
        tiles = [jnp.zeros((tokens, 128), F32) for _ in range(span // 128)]
        for h in range(group):
            first = size * h // 128
            last = (size * h + size - 1) // 128
            wide_here = (last - first + 1) * 128
            lanes = pl.ds(pl.multiple_of(left + first * 128, 128), wide_here)
            spot = iota((tokens, wide_here), 1) + first * 128
            mine = (spot >= size * h) & (spot < size * (h + 1))
            q = query[s, :, lanes]
            q = jnp.where(mine, q, jnp.zeros_like(q))
            keys = kv[s, :, lanes]
            values = kv[s, :, pl.ds(pl.multiple_of(left + width + first * 128, 128), wide_here)]
            scores = mm_t(q, keys) * size ** (-0.5) + bias[g * group + h].astype(F32)
            weights = jnp.exp(scores - jnp.max(scores, axis=-1, keepdims=True))
            sums = jnp.sum(weights, axis=-1, keepdims=True)
            part = jnp.where(mine, mm(weights.astype(BF), values) / sums, 0.0)
            for t in range(first, last + 1):
                tiles[t] = tiles[t] + part[:, (t - first) * 128 : (t - first + 1) * 128]
        for t, tile in enumerate(tiles):
            attended[s, :, pl.ds(pl.multiple_of(left + t * 128, 128), 128)] = tile
        return carry

    lax.fori_loop(0, seeds * (heads // group), step, 0)


def remote(source, target, send, arrive, **place):
    return pltpu.make_async_remote_copy(
        src_ref=source, dst_ref=target, send_sem=send, recv_sem=arrive,
        device_id=place, device_id_type=pl.DeviceIdType.MESH,
    )


def main_kernel(
    count, groups,
    x, atom_bias, index, cond, enc_project, enc_mix, pool, bias_hbm, project_hbm, mix_hbm, wide_hbm,
    down_hbm, spread_w,
    enc, state_out, spread_out,
    packed, mixed, residual, everyone, kv, query, gate, attended, bias, project, mix, wide, down,
    sems, bias_send, bias_recv, right_send, right_recv, left_send, left_recv, twin_send, twin_recv,
):
    tok = lax.axis_index("tok")
    seed = lax.axis_index("seed")
    chips = count // 2
    chip = tok // 2
    twin = tok + 1 - 2 * (tok % 2)
    hops = chips - 1

    barrier = pltpu.get_barrier_semaphore()

    def greet(**place):
        pl.semaphore_signal(
            barrier, inc=1, device_id=place, device_id_type=pl.DeviceIdType.MESH
        )

    greet(tok=twin)
    for k in range(1, groups):
        greet(seed=lax.rem(seed + k, groups))

    @pl.when(chip > 0)
    def _():
        greet(tok=tok - 2)

    @pl.when(chip < chips - 1)
    def _():
        greet(tok=tok + 2)

    has_left = jnp.where(chip > 0, 1, 0)
    has_right = jnp.where(chip < chips - 1, 1, 0)
    pl.semaphore_wait(barrier, groups + has_left + has_right)

    share = bias_hbm.shape[0]
    slot = bias.at[pl.ds(seed * share, share)]
    bias_copies = [
        remote(bias_hbm, slot, bias_send.at[k - 1], bias_recv.at[k - 1],
               seed=lax.rem(seed + k, groups))
        for k in range(1, groups)
    ]
    for copy in bias_copies:
        copy.start()
    loads = [
        pltpu.make_async_copy(source, target, sems.at[i])
        for i, (source, target) in enumerate(
            (
                (bias_hbm, slot), (project_hbm, project), (mix_hbm, mix), (wide_hbm, wide),
                (down_hbm, down),
            )
        )
    ]
    for load in loads:
        load.start()

    seeds, total, _ = x.shape
    inner = mixed.shape[1] - 2 * RIM
    low, high = limits(tok, count, HALO, inner, total)
    encode(low, high, x, atom_bias, index, cond, enc_project, enc_mix, pool, enc, residual, packed, mixed)

    tokens, width = cond.shape
    everyone[tok] = layer_norm(residual[...]).astype(BF)

    def to_right(k):
        piece = everyone.at[tok - 2 * k]
        return remote(piece, piece, right_send.at[k], right_recv.at[k], tok=tok + 2)

    def to_left(k):
        piece = everyone.at[tok + 2 * k]
        return remote(piece, piece, left_send.at[k], left_recv.at[k], tok=tok - 2)

    def to_twin(k):
        piece = everyone.at[tok + 2 * k]
        return remote(piece, piece, twin_send.at[hops + k], twin_recv.at[hops + k], tok=twin)

    @pl.when(chip < chips - 1)
    def _():
        to_right(0).start()

    @pl.when(chip > 0)
    def _():
        to_left(0).start()

    to_twin(0).start()

    loads[1].wait()
    own = everyone[tok].reshape(seeds * tokens, width)
    query[...] = mm(own, project[:, :width]).astype(BF).reshape(seeds, tokens, width)
    gate[...] = jax.nn.sigmoid(mm(own, project[:, 3 * width :]))

    def keys_values(place):
        part = everyone[place].reshape(seeds * tokens, width)
        first = pl.multiple_of(place * tokens, tokens)
        for at in range(0, 2 * width, width):
            piece = mm(part, project[:, width + at : 2 * width + at]).astype(BF)
            kv[:, pl.ds(first, tokens), at : at + width] = piece.reshape(seeds, tokens, width)

    keys_values(tok)
    to_twin(0).wait_recv()
    keys_values(twin)
    for k in range(1, hops + 1):
        from_left = chip - k >= 0
        from_right = chip + k < chips

        @pl.when(from_left)
        def _(k=k):
            to_right(k - 1).wait_recv()
            to_twin(-k).start()
            if k < hops:

                @pl.when(chip < chips - 1)
                def _():
                    to_right(k).start()

        @pl.when(from_right)
        def _(k=k):
            to_left(k - 1).wait_recv()
            to_twin(k).start()
            if k < hops:

                @pl.when(chip > 0)
                def _():
                    to_left(k).start()

        @pl.when(from_left)
        def _(k=k):
            keys_values(tok - 2 * k)

        @pl.when(from_right)
        def _(k=k):
            keys_values(tok + 2 * k)

        @pl.when(from_left)
        def _(k=k):
            to_twin(-k).wait_recv()
            keys_values(twin - 2 * k)

        @pl.when(from_right)
        def _(k=k):
            to_twin(k).wait_recv()
            keys_values(twin + 2 * k)

    loads[0].wait()
    for copy in bias_copies:
        copy.wait()
    attend(bias, query, kv, attended)

    loads[2].wait()
    gated = (attended[...].reshape(seeds * tokens, width) * gate[...]).astype(BF)
    state = residual[...].reshape(seeds * tokens, width) + mm(gated, mix[...])
    part = layer_norm(state).astype(BF)
    loads[3].wait()
    hidden = down.shape[0]
    part = (jax.nn.silu(mm(part, wide[:, :hidden])) * mm(part, wide[:, hidden:])).astype(BF)
    loads[4].wait()
    state = (state + mm(part, down[...])).astype(BF)
    state_out[...] = state.reshape(seeds, tokens, width)
    spread_out[...] = mm(state, spread_w[...]).astype(BF).reshape(spread_out.shape)

    to_twin(0).wait_send()
    for k in range(hops):

        @pl.when((chip - k >= 0) & (chip < chips - 1))
        def _(k=k):
            to_right(k).wait_send()

        @pl.when((chip + k < chips) & (chip > 0))
        def _(k=k):
            to_left(k).wait_send()

        @pl.when(chip - k - 1 >= 0)
        def _(k=k):
            to_twin(-k - 1).wait_send()

        @pl.when(chip + k + 1 < chips)
        def _(k=k):
            to_twin(k + 1).wait_send()


def decode_kernel(count, enc, spread, index, bias, project, mix, out, decoded, packed, mixed):
    seeds, rows, width = enc.shape
    inner = out.shape[1]
    low, high = limits(lax.axis_index("tok"), count, RIM, inner, rows)
    picker = (index[...] == iota((spread.shape[1], rows), 0) - EDGE).astype(BF)
    chunk = rows // 3
    for s in range(seeds):
        for at in range(0, rows, chunk):
            carried = lax.dot_general(
                picker[:, at : at + chunk], spread[s], (((0,), (0,)), ((), ())),
                preferred_element_type=F32,
            )
            part = (enc[s, at : at + chunk, :].astype(F32) + carried).astype(BF)
            decoded[s, at : at + chunk, :] = part
            part = layer_norm(part.astype(F32)).astype(BF)
            packed[s, at : at + chunk, : 3 * width] = mm(part, project[...]).astype(BF)
    packed[:, :, 3 * width :] = jnp.ones((seeds, rows, width), BF)
    window_attention(packed, bias, mixed, inner // QUERY_BLOCK, RIM - 48, low, high, 2)
    for s in range(seeds):
        for at in range(0, inner, 256):
            base = decoded[s, RIM + at : RIM + at + 256, :].astype(F32)
            out[s, at : at + 256, :] = (base + mm(mixed[s, at : at + 256, :], mix[...])).astype(BF)


PARAMS = pltpu.CompilerParams(vmem_limit_bytes=50 * 1024 * 1024)


def exchange(to_above, to_below):
    count = lax.axis_size("tok")
    above = [(i, i + 1) for i in range(count - 1)]
    below = [(target, source) for source, target in above]
    return lax.ppermute(to_above, "tok", above), lax.ppermute(to_below, "tok", below)


def per_device(
    atom_feats, atom_index, token_cond, pair_bias, atom_bias_enc, atom_bias_dec,
    enc_project, enc_mix, pool_weight, token_project, token_mix, swiglu_in, swiglu_out,
    spread_weight, dec_project, dec_mix,
):
    atoms, seeds, width = atom_feats.shape
    tokens, token_width = token_cond.shape
    atom_heads, window = atom_bias_enc.shape[1:]
    count = lax.axis_size("tok")
    tok = lax.axis_index("tok")
    relative = atom_index - tok * tokens
    x = atom_feats.transpose(1, 0, 2)

    def by_head(bias):
        parts = bias.reshape(atoms // QUERY_BLOCK, QUERY_BLOCK, atom_heads, window)
        return parts.transpose(0, 2, 1, 3).reshape(atoms * atom_heads, window)

    enc_bias = by_head(atom_bias_enc)
    dec_bias = by_head(atom_bias_dec)

    def parcel(at, at_rim):
        row = jnp.zeros((8, width), BF).at[0, :RIM].set(relative[at_rim : at_rim + RIM].astype(BF))
        rim = atom_heads * at_rim
        return jnp.concatenate(
            [
                x[:, at : at + HALO].reshape(seeds * HALO, width),
                enc_bias[rim : rim + atom_heads * RIM],
                row,
            ]
        )

    def unpack(parcel):
        cut = seeds * HALO
        end = cut + atom_heads * RIM
        return (
            parcel[:cut].reshape(seeds, HALO, width),
            parcel[cut:end],
            parcel[end, :RIM].astype(jnp.int32),
        )

    lower, upper = exchange(parcel(atoms - HALO, atoms - RIM), parcel(0, 0))
    lower_x, lower_bias, lower_index = unpack(lower)
    upper_x, upper_bias, upper_index = unpack(upper)
    x_ext = jnp.concatenate([lower_x, x, upper_x], axis=1)
    bias_ext = jnp.concatenate([lower_bias, enc_bias, upper_bias])
    lower_index = jnp.where(tok == 0, MISSING, lower_index - tokens)
    upper_index = jnp.where(tok == count - 1, MISSING, upper_index + tokens)
    index_ext = jnp.concatenate([lower_index, relative, upper_index])[None]
    rows = atoms + 2 * RIM

    groups = lax.axis_size("seed")
    hops = max(count // 2 - 1, 1)
    vmem = pl.BlockSpec(memory_space=pltpu.VMEM)
    hbm = pl.BlockSpec(memory_space=pl.ANY)
    flat = (seeds, tokens, token_width)
    dma = pltpu.SemaphoreType.DMA
    encoded, state, spread = pl.pallas_call(
        functools.partial(main_kernel, count, groups),
        out_shape=(
            jax.ShapeDtypeStruct((seeds, rows, width), BF),
            jax.ShapeDtypeStruct(flat, BF),
            jax.ShapeDtypeStruct((seeds, tokens, width), BF),
        ),
        in_specs=[vmem] * 7 + [hbm] * 5 + [vmem],
        scratch_shapes=[
            pltpu.VMEM((seeds, atoms + 2 * HALO, 4 * width), BF),
            pltpu.VMEM((seeds, rows, width), BF),
            pltpu.VMEM(flat, F32),
            pltpu.VMEM((count,) + flat, BF),
            pltpu.VMEM((seeds, count * tokens, 2 * token_width), BF),
            pltpu.VMEM(flat, BF),
            pltpu.VMEM((seeds * tokens, token_width), F32),
            pltpu.VMEM(flat, F32),
            pltpu.VMEM((HEADS,) + pair_bias.shape[1:], BF),
            pltpu.VMEM(token_project.shape, BF),
            pltpu.VMEM(token_mix.shape, BF),
            pltpu.VMEM(swiglu_in.shape, BF),
            pltpu.VMEM(swiglu_out.shape, BF),
            dma((5,)),
            dma((groups - 1,)),
            dma((groups - 1,)),
            dma((hops,)),
            dma((hops,)),
            dma((hops,)),
            dma((hops,)),
            dma((2 * hops + 1,)),
            dma((2 * hops + 1,)),
        ],
        compiler_params=pltpu.CompilerParams(
            vmem_limit_bytes=56 * 1024 * 1024, collective_id=0, has_side_effects=True
        ),
        name="main",
    )(x_ext, bias_ext, index_ext, token_cond, enc_project, enc_mix, pool_weight, pair_bias,
      token_project, token_mix, swiglu_in, swiglu_out, spread_weight)

    low_rows, high_rows = exchange(spread[:, tokens - EDGE :], spread[:, :EDGE])
    spread_ext = jnp.concatenate([low_rows, spread, high_rows], axis=1)
    update = pl.pallas_call(
        functools.partial(decode_kernel, count),
        out_shape=jax.ShapeDtypeStruct((seeds, atoms, width), BF),
        scratch_shapes=[
            pltpu.VMEM((seeds, rows, width), BF),
            pltpu.VMEM((seeds, rows, 4 * width), BF),
            pltpu.VMEM((seeds, atoms, width), BF),
        ],
        compiler_params=PARAMS,
        name="decode",
    )(encoded, spread_ext, index_ext, dec_bias, dec_project, dec_mix)
    return state.transpose(1, 0, 2), update.transpose(1, 0, 2)


def solution(mesh):
    placed = (
        P("tok", "seed", None),
        P("tok"),
        P("tok", None),
        P("seed", "tok", None),
        P("tok", None, None),
        P("tok", None, None),
    ) + (P(),) * 10
    return jax.shard_map(
        per_device,
        mesh=mesh,
        in_specs=placed,
        out_specs=(P("tok", "seed", None), P("tok", "seed", None)),
        check_vma=False,
    )
```

time: 228 us -> 104 us (0.46)
  waiting for transfers between devices: 97.4 us -> 5.9 us
  Pallas kernels: 96.6 us -> 76.5 us
  between operations: 14.3 us -> 0.89 us
    all_gather x2 -> x0, waiting for transfers between devices: 90.8 us -> none  [the longest x1 53 us: per_device(): whole_bias = lax.all_gather(pair_bias, 'seed', axis=0, tiled=True)]
    pallas_call x1, Pallas kernels: 32.7 us -> 10.6 us  [per_device(): pl.pallas_call(functools.partial(decode_kernel, count), out_shape=jax.Sha...]
    pallas_call x2 -> x1, Pallas kernels: 63.9 us -> 65.9 us  [per_device(): pl.pallas_call(functools.partial(main_kernel, count, groups), out_shape=(...]
  transfers between devices with their start and end apart: 6 -> 4, of which waited for: 4 -> 2; matrix products, arithmetic and copies ran while one was open for 1% -> 1% of each run, Pallas kernels for 0% -> 0%
where the time goes in v2:
time: 104 us
  Pallas kernels  76.5 us (74%)
  starting transfers between devices  11.7 us (11%)
  waiting for transfers between devices  5.9 us (6%)
  local copies, waits for them, and re-layouts  5.77 us (6%)
  other arithmetic  2.8 us (3%)
    pallas_call x1, Pallas kernels, per_device(): pl.pallas_call(functools.partial(main_kernel, count, groups), out_shape=(...  65.9 us
    pallas_call x1, Pallas kernels, per_device(): pl.pallas_call(functools.partial(decode_kernel, count), out_shape=jax.Sha...  10.6 us
    ppermute x2, starting transfers between devices, exchange(): lax.ppermute(to_above, 'tok', above)  7.81 us
    ppermute x2, waiting for transfers between devices, exchange(): lax.ppermute(to_below, 'tok', below)  5.9 us
    ppermute x2, starting transfers between devices, exchange(): lax.ppermute(to_below, 'tok', below)  3.84 us
    unnamed x19, local copies, waits for them, and re-layouts  2.59 us
  transfers between devices with their start and end apart: 4, of which 2 were waited for; matrix products, arithmetic and copies ran while one was open for 1% of the time, Pallas kernels for 0%

profile of v2, /device:TPU:1, one launch (start us, length us, event | category | flops | bytes accessed | tf_op | source)
XLA Modules:
  0.0 103.6 jit_solution(18379193196589781162)
XLA Ops:
  0.6 0.0 copy-start.5
  0.6 0.7 fusion.8
  1.4 0.1 slice_bitcast_fusion.1
  1.5 1.4 %copy.27 = bf16[32,32,4,128]{3,1,2,0:T(8,128)(2,1)S(1)} copy(bf16[32,32,4,128]{3,2,1,0:T(4,128)(2,1)} %bitcast.34) | data formatting | bytes 2097152 | tf_op jit(solution)/shard_map/reshape | solution.py:391
  2.9 0.0 copy-done.5
  2.9 0.1 copy.26
  3.1 4.6 %collective-permute-start = (bf16[520,128]{1,0:T(8,128)(2,1)S(1)}, bf16[520,128]{1,0:T(8,128)(2,1)S(1)}, u32[]{:S(2)}, u32[]{:S(2)}) collective-permute-start(bf16[520,128]{1,0:T(8,128)(2,1)S(1)} %fusion.2), channel_id=1, source_target_pairs={{0,1},{1,2},{2,3},{3,4},{4,5},{5,6},{6,7},{8,9},{9,10},{10,11},{11... | collective-permute-start | bytes 399368 | tf_op jit(solution)/shard_map/ppermute | solution.py:374
  7.7 1.9 %collective-permute-start.1 = (bf16[520,128]{1,0:T(8,128)(2,1)S(1)}, bf16[520,128]{1,0:T(8,128)(2,1)S(1)}, u32[]{:S(2)}, u32[]{:S(2)}) collective-permute-start(bf16[520,128]{1,0:T(8,128)(2,1)S(1)} %fusion.3), channel_id=1, source_target_pairs={{1,0},{2,1},{3,2},{4,3},{5,4},{6,5},{7,6},{9,8},{10,9},{11,10},{12... | collective-permute-start | bytes 399368 | tf_op jit(solution)/shard_map/ppermute | solution.py:374
  9.6 0.0 collective-permute-done
  9.6 4.3 %collective-permute-done.1 = bf16[520,128]{1,0:T(8,128)(2,1)S(1)} collective-permute-done((bf16[520,128]{1,0:T(8,128)(2,1)S(1)}, bf16[520,128]{1,0:T(8,128)(2,1)S(1)}, u32[]{:S(2)}, u32[]{:S(2)}) %collective-permute-start.1) | collective-permute-done | bytes 133152 | tf_op jit(solution)/shard_map/ppermute | solution.py:374
  14.0 0.1 concatenate.26
  14.1 0.6 broadcast_in_dim.9.index
  14.7 0.9 pad_maximum_fusion.1.x
  15.6 1.1 %pad_maximum_fusion.atom_bias = bf16[4608,128]{1,0:T(8,128)(2,1)} fusion(bf16[256,128]{1,0:T(8,128)(2,1)S(1)} %get-tuple-element.44, bf16[4096,128]{1,0:T(8,128)(2,1)S(1)} %bitcast.31, bf16[256,128]{1,0:T(8,128)(2,1)S(1)} %get-tuple-element.42), kind=kLoop, calls=%fused_computation | loop fusion | flops 3538944 | bytes 2359296 | tf_op jit(solution)/shard_map/concatenate | solution.py:421
  16.7 65.9 %main.1 = (bf16[2,1152,128]{2,1,0:T(8,128)(2,1)}, bf16[2,128,768]{2,1,0:T(8,128)(2,1)}, bf16[2,128,128]{2,1,0:T(8,128)(2,1)}) custom-call(bf16[2,1280,128]{2,1,0:T(8,128)(2,1)} %pad_maximum_fusion.1.x, bf16[4608,128]{1,0:T(8,128)(2,1)} %pad_maximum_fusion.atom_bias, s32[1,1152]{1,0:T(1,128)} %broadcast_in_dim.9.index, bf16[128,768]{1,0:T(8,128)(2,1)} %cond.1, ...), custom_call_target="tpu_custom_call" | custom-call | tf_op jit(solution)/shard_map/main/pallas_call | solution.py:433
  82.7 0.0 copy-start.6
  82.7 0.7 fusion.14
  83.4 3.2 %collective-permute-start.2 = (bf16[2,8,128]{2,1,0:T(8,128)(2,1)S(1)}, bf16[2,8,128]{2,1,0:T(8,128)(2,1)S(1)}, u32[]{:S(2)}, u32[]{:S(2)}) collective-permute-start(bf16[2,8,128]{2,1,0:T(8,128)(2,1)S(1)} %get-tuple-element.46), channel_id=1, source_target_pairs={{0,1},{1,2},{2,3},{3,4},{4,5},{5,6},{6,7},{8,9},{9,10},{10,11},{11... | collective-permute-start | bytes 12296 | tf_op jit(solution)/shard_map/ppermute | solution.py:374
  86.6 1.9 %collective-permute-start.3 = (bf16[2,8,128]{2,1,0:T(8,128)(2,1)S(1)}, bf16[2,8,128]{2,1,0:T(8,128)(2,1)S(1)}, u32[]{:S(2)}, u32[]{:S(2)}) collective-permute-start(bf16[2,8,128]{2,1,0:T(8,128)(2,1)S(1)} %get-tuple-element.47), channel_id=1, source_target_pairs={{1,0},{2,1},{3,2},{4,3},{5,4},{6,5},{7,6},{9,8},{10,9},{11,10},{12... | collective-permute-start | bytes 12296 | tf_op jit(solution)/shard_map/ppermute | solution.py:374
  88.6 0.0 copy-done.4
  88.6 0.0 copy-start.7
  88.6 0.0 copy-start
  88.6 0.0 copy-start.1
  88.6 0.0 copy-start.2
  88.6 0.0 copy-start.3
  88.6 0.2 copy.20
  88.9 0.0 copy-done.6
  88.9 1.2 %copy.21 = bf16[128,2,768]{2,1,0:T(2,128)(2,1)} copy(bf16[128,2,768]{2,0,1:T(8,128)(2,1)S(1)} %bitcast.36) | data formatting | bytes 786432
  90.0 0.0 collective-permute-done.2
  90.0 1.5 %collective-permute-done.3 = bf16[2,8,128]{2,1,0:T(8,128)(2,1)S(1)} collective-permute-done((bf16[2,8,128]{2,1,0:T(8,128)(2,1)S(1)}, bf16[2,8,128]{2,1,0:T(8,128)(2,1)S(1)}, u32[]{:S(2)}, u32[]{:S(2)}) %collective-permute-start.3) | collective-permute-done | bytes 4128 | tf_op jit(solution)/shard_map/ppermute | solution.py:374
  91.6 10.6 %decode.1 = bf16[2,1024,128]{2,1,0:T(8,128)(2,1)S(1)} custom-call(bf16[2,1152,128]{2,1,0:T(8,128)(2,1)S(1)} %copy-done, bf16[2,144,128]{2,1,0:T(8,128)(2,1)S(1)} %pad_maximum_fusion.2.spread, s32[1,1152]{1,0:T(1,128)S(1)} %copy-done.2, bf16[4096,128]{1,0:T(8,128)(2,1)S(1)} %bitcast.28, bf16[128,384]{1,0:T(8,128)(2,1)S(1)} %copy-done.1, ...), custom_call_target="tpu_custom_call" | custom-call | tf_op jit(solution)/shard_map/decode/pallas_call | solution.py:474
  102.2 1.3 %copy.22 = bf16[1024,2,128]{2,1,0:T(2,128)(2,1)} copy(bf16[1024,2,128]{2,0,1:T(8,128)(2,1)S(1)} %bitcast.29) | data formatting | bytes 1048576
  (15 shorter events, 0.1 us)
Async XLA Ops:
  0.6 2.3 %copy-start.5 = (bf16[1024,2,128]{2,1,0:T(2,128)(2,1)S(1)}, bf16[1024,2,128]{2,1,0:T(2,128)(2,1)}, u32[]{:S(2)}) copy-start(bf16[1024,2,128]{2,1,0:T(2,128)(2,1)} %param.20) | copy-start | bytes 1572868
  3.1 6.6 %collective-permute-start = (bf16[520,128]{1,0:T(8,128)(2,1)S(1)}, bf16[520,128]{1,0:T(8,128)(2,1)S(1)}, u32[]{:S(2)}, u32[]{:S(2)}) collective-permute-start(bf16[520,128]{1,0:T(8,128)(2,1)S(1)} %fusion.2), channel_id=1, source_target_pairs={{0,1},{1,2},{2,3},{3,4},{4,5},{5,6},{6,7},{8,9},{9,10},{10,11},{11... | collective-permute-start | bytes 399368 | tf_op jit(solution)/shard_map/ppermute | solution.py:374
  7.7 6.3 %collective-permute-start.1 = (bf16[520,128]{1,0:T(8,128)(2,1)S(1)}, bf16[520,128]{1,0:T(8,128)(2,1)S(1)}, u32[]{:S(2)}, u32[]{:S(2)}) collective-permute-start(bf16[520,128]{1,0:T(8,128)(2,1)S(1)} %fusion.3), channel_id=1, source_target_pairs={{1,0},{2,1},{3,2},{4,3},{5,4},{6,5},{7,6},{9,8},{10,9},{11,10},{12... | collective-permute-start | bytes 399368 | tf_op jit(solution)/shard_map/ppermute | solution.py:374
  16.7 71.9 %copy-start.4 = (bf16[1024,4,128]{2,1,0:T(4,128)(2,1)S(1)}, bf16[1024,4,128]{2,1,0:T(4,128)(2,1)}, u32[]{:S(2)}) copy-start(bf16[1024,4,128]{2,1,0:T(4,128)(2,1)} %param.25) | copy-start | bytes 3145732
  82.7 6.2 %copy-start.6 = (bf16[2,128,768]{2,1,0:T(8,128)(2,1)S(1)}, bf16[2,128,768]{2,1,0:T(8,128)(2,1)}, u32[]{:S(2)}) copy-start(bf16[2,128,768]{2,1,0:T(8,128)(2,1)} %get-tuple-element.29) | copy-start | bytes 1179652
  83.4 6.6 %collective-permute-start.2 = (bf16[2,8,128]{2,1,0:T(8,128)(2,1)S(1)}, bf16[2,8,128]{2,1,0:T(8,128)(2,1)S(1)}, u32[]{:S(2)}, u32[]{:S(2)}) collective-permute-start(bf16[2,8,128]{2,1,0:T(8,128)(2,1)S(1)} %get-tuple-element.46), channel_id=1, source_target_pairs={{0,1},{1,2},{2,3},{3,4},{4,5},{5,6},{6,7},{8,9},{9,10},{10,11},{11... | collective-permute-start | bytes 12296 | tf_op jit(solution)/shard_map/ppermute | solution.py:374
  86.6 4.9 %collective-permute-start.3 = (bf16[2,8,128]{2,1,0:T(8,128)(2,1)S(1)}, bf16[2,8,128]{2,1,0:T(8,128)(2,1)S(1)}, u32[]{:S(2)}, u32[]{:S(2)}) collective-permute-start(bf16[2,8,128]{2,1,0:T(8,128)(2,1)S(1)} %get-tuple-element.47), channel_id=1, source_target_pairs={{1,0},{2,1},{3,2},{4,3},{5,4},{6,5},{7,6},{9,8},{10,9},{11,10},{12... | collective-permute-start | bytes 12296 | tf_op jit(solution)/shard_map/ppermute | solution.py:374
  88.6 3.0 %copy-start.7 = (bf16[2,128,128]{2,1,0:T(8,128)(2,1)S(1)}, bf16[2,128,128]{2,1,0:T(8,128)(2,1)}, u32[]{:S(2)}) copy-start(bf16[2,128,128]{2,1,0:T(8,128)(2,1)} %get-tuple-element.31) | copy-start | bytes 196612
  88.6 3.0 %copy-start = (bf16[2,1152,128]{2,1,0:T(8,128)(2,1)S(1)}, bf16[2,1152,128]{2,1,0:T(8,128)(2,1)}, u32[]{:S(2)}) copy-start(bf16[2,1152,128]{2,1,0:T(8,128)(2,1)} %get-tuple-element.30.enc) | copy-start | bytes 1769476
  88.6 3.0 %copy-start.1 = (bf16[128,384]{1,0:T(8,128)(2,1)S(1)}, bf16[128,384]{1,0:T(8,128)(2,1)}, u32[]{:S(2)}) copy-start(bf16[128,384]{1,0:T(8,128)(2,1)} %project.1) | copy-start | bytes 294916
  88.6 3.0 %copy-start.2 = (s32[1,1152]{1,0:T(1,128)S(1)}, s32[1,1152]{1,0:T(1,128)}, u32[]{:S(2)}) copy-start(s32[1,1152]{1,0:T(1,128)} %broadcast_in_dim.9.index) | copy-start | bytes 13828
  88.6 3.0 %copy-start.3 = (bf16[128,128]{1,0:T(8,128)(2,1)S(1)}, bf16[128,128]{1,0:T(8,128)(2,1)}, u32[]{:S(2)}) copy-start(bf16[128,128]{1,0:T(8,128)(2,1)} %mix.1) | copy-start | bytes 98308

commit v3 on v2

--- a/solution.py
+++ b/solution.py
@@ -13,7 +13,7 @@
 NEGATIVE = -1000000000.0
 HALO = 128
 RIM = 64
-EDGE = 8
+EDGE = 16
 MISSING = -1000
 BF = jnp.bfloat16
 F32 = jnp.float32
@@ -37,11 +37,11 @@
     return lax.broadcasted_iota(jnp.int32, shape, dim)
 
 
-def window_attention(packed, bias, mixed, blocks, key_base, low, high, group):
+def window_attention(packed, bias, mixed, first_row, blocks, low, high, group):
     seeds, _, quad = packed.shape
     width = quad // 4
     window = bias.shape[1]
-    heads = bias.shape[0] // mixed.shape[1]
+    heads = bias.shape[0] // (QUERY_BLOCK * blocks)
     size = width // heads
     rows = QUERY_BLOCK * heads
     margin = (window - QUERY_BLOCK) // 2
@@ -52,7 +52,7 @@
         scores, places = [], []
         for g in range(group):
             j = i * group + g
-            start = pl.multiple_of(key_base + QUERY_BLOCK * j, 16)
+            start = pl.multiple_of(first_row - margin + QUERY_BLOCK * j, 16)
             term = bias[pl.ds(pl.multiple_of(rows * j, rows), rows), :].astype(F32)
             spot = lane + start
             term = jnp.where((spot >= low) & (spot < high), term, NEGATIVE)
@@ -76,41 +76,36 @@
             total = part[:QUERY_BLOCK]
             for h in range(1, heads):
                 total = jnp.where(column == h, part[QUERY_BLOCK * h : QUERY_BLOCK * (h + 1)], total)
-            first = pl.multiple_of(QUERY_BLOCK * j, QUERY_BLOCK)
+            first = pl.multiple_of(first_row + QUERY_BLOCK * j, QUERY_BLOCK)
             mixed[s, pl.ds(first, QUERY_BLOCK), :] = total.astype(BF)
         return carry
 
     lax.fori_loop(0, blocks // group, step, 0)
 
 
-def limits(tok, count, front, inner, total):
-    low = jnp.where(tok == 0, front, 0)
-    high = jnp.where(tok == count - 1, front + inner, total)
-    return low, high
-
-
-def encode(low, high, x, bias, index, cond, project, mix, pool, enc, residual, packed, mixed):
+def packed_rows(packed, project, source, begin, end, chunk):
+    seeds, _, quad = packed.shape
+    used = quad // 4 * 3
+    for s in range(seeds):
+        for at in range(begin, end, chunk):
+            part = layer_norm(source[s, at : at + chunk, :].astype(F32)).astype(BF)
+            packed[s, at : at + chunk, :used] = mm(part, project[...]).astype(BF)
+
+
+def pool_tokens(x, index, cond, mix, pool, enc, residual, mixed):
     seeds, total, width = x.shape
-    rows = mixed.shape[1]
-    for s in range(seeds):
-        for at in range(0, total, 256):
-            part = layer_norm(x[s, at : at + 256, :].astype(F32)).astype(BF)
-            packed[s, at : at + 256, : 3 * width] = mm(part, project[...]).astype(BF)
-    packed[:, :, 3 * width :] = jnp.ones((seeds, total, width), BF)
-    window_attention(packed, bias, mixed, rows // QUERY_BLOCK, HALO - RIM - 48, low, high, 2)
     tokens = cond.shape[0]
-    chosen = index[...] == iota((tokens, rows), 0)
+    chosen = index == iota((tokens, total), 0)
     counts = jnp.sum(chosen.astype(F32), axis=1, keepdims=True)
     chosen = chosen.astype(BF)
-    chunk = rows // 3
     for s in range(seeds):
         sums = jnp.zeros(residual.shape[1:], F32)
-        for at in range(0, rows, chunk):
-            base = x[s, at + HALO - RIM : at + HALO - RIM + chunk, :].astype(F32)
-            part = (base + mm(mixed[s, at : at + chunk, :], mix[...])).astype(BF)
-            enc[s, at : at + chunk, :] = part
+        for at in range(0, total, 256):
+            base = x[s, at : at + 256, :].astype(F32)
+            part = (base + mm(mixed[s, at : at + 256, :], mix[...])).astype(BF)
+            enc[s, at : at + 256, :] = part
             lifted = jnp.maximum(mm(part, pool[...]), 0.0).astype(BF)
-            sums = sums + mm(chosen[:, at : at + chunk], lifted)
+            sums = sums + mm(chosen[:, at : at + 256], lifted)
         residual[s] = cond[...].astype(F32) + sums / counts
 
 
@@ -159,15 +154,18 @@
 
 def main_kernel(
     count, groups,
-    x, atom_bias, index, cond, enc_project, enc_mix, pool, bias_hbm, project_hbm, mix_hbm, wide_hbm,
-    down_hbm, spread_w,
-    enc, state_out, spread_out,
+    atoms_in, enc_bias_hbm, index_in, first_index, last_index, cond, enc_project, enc_mix, pool,
+    bias_hbm, project_hbm, mix_hbm, wide_hbm, down_hbm, spread_w, dec_bias_hbm, dec_project, dec_mix,
+    state_out, out,
+    x, atom_bias, low_index, high_index, enc, decoded, spread, dec_bias,
     packed, mixed, residual, everyone, kv, query, gate, attended, bias, project, mix, wide, down,
     sems, bias_send, bias_recv, right_send, right_recv, left_send, left_recv, twin_send, twin_recv,
+    up_send, up_recv, down_send, down_recv,
 ):
     tok = lax.axis_index("tok")
     seed = lax.axis_index("seed")
     chips = count // 2
+    inner_tokens = cond.shape[0]
     chip = tok // 2
     twin = tok + 1 - 2 * (tok % 2)
     hops = chips - 1
@@ -191,9 +189,67 @@
     def _():
         greet(tok=tok + 2)
 
+    side = tok - 1 + 2 * (tok % 2)
+    has_side = (side >= 0) & (side < count)
+
+    @pl.when(has_side)
+    def _():
+        greet(tok=side)
+
     has_left = jnp.where(chip > 0, 1, 0)
     has_right = jnp.where(chip < chips - 1, 1, 0)
-    pl.semaphore_wait(barrier, groups + has_left + has_right)
+    pl.semaphore_wait(barrier, groups + has_left + has_right + jnp.where(has_side, 1, 0))
+
+    seeds, inner, width = atoms_in.shape
+    total = inner + 2 * HALO
+    heads = enc_bias_hbm.shape[0] // inner
+    rim = heads * RIM
+    own_bias = heads * inner
+    has_below = tok > 0
+    has_above = tok < count - 1
+
+    def up(i, source, target):
+        return remote(source, target, up_send.at[i], up_recv.at[i], tok=tok + 1)
+
+    def below(i, source, target):
+        return remote(source, target, down_send.at[i], down_recv.at[i], tok=tok - 1)
+
+    upward = [
+        (0, atoms_in.at[:, pl.ds(inner - HALO, HALO)], x.at[:, pl.ds(0, HALO)]),
+        (1, enc_bias_hbm.at[pl.ds(own_bias - rim, rim)], atom_bias.at[pl.ds(0, rim)]),
+        (2, last_index, low_index),
+    ]
+    downward = [
+        (0, atoms_in.at[:, pl.ds(0, HALO)], x.at[:, pl.ds(HALO + inner, HALO)]),
+        (1, enc_bias_hbm.at[pl.ds(0, rim)], atom_bias.at[pl.ds(rim + own_bias, rim)]),
+        (2, first_index, high_index),
+    ]
+    edge_up = (3, spread.at[:, pl.ds(inner_tokens, EDGE)], spread.at[:, pl.ds(0, EDGE)])
+    edge_down = (3, spread.at[:, pl.ds(EDGE, EDGE)], spread.at[:, pl.ds(EDGE + inner_tokens, EDGE)])
+
+    @pl.when(has_above)
+    def _():
+        for part in upward:
+            up(*part).start()
+
+    @pl.when(has_below)
+    def _():
+        for part in downward:
+            below(*part).start()
+
+    @pl.when(tok == 0)
+    def _():
+        x[:, :HALO] = jnp.zeros((seeds, HALO, width), BF)
+        atom_bias[:rim] = jnp.zeros((rim, width), BF)
+        low_index[...] = jnp.full(low_index.shape, MISSING, jnp.int32)
+        spread[:, :EDGE] = jnp.zeros((seeds, EDGE, width), BF)
+
+    @pl.when(tok == count - 1)
+    def _():
+        x[:, HALO + inner :] = jnp.zeros((seeds, HALO, width), BF)
+        atom_bias[rim + own_bias :] = jnp.zeros((rim, width), BF)
+        high_index[...] = jnp.full(high_index.shape, MISSING, jnp.int32)
+        spread[:, EDGE + inner_tokens :] = jnp.zeros((seeds, EDGE, width), BF)
 
     share = bias_hbm.shape[0]
     slot = bias.at[pl.ds(seed * share, share)]
@@ -209,17 +265,41 @@
         for i, (source, target) in enumerate(
             (
                 (bias_hbm, slot), (project_hbm, project), (mix_hbm, mix), (wide_hbm, wide),
-                (down_hbm, down),
+                (down_hbm, down), (dec_bias_hbm, dec_bias),
+                (enc_bias_hbm, atom_bias.at[pl.ds(rim, own_bias)]),
             )
         )
     ]
     for load in loads:
         load.start()
 
-    seeds, total, _ = x.shape
-    inner = mixed.shape[1] - 2 * RIM
-    low, high = limits(tok, count, HALO, inner, total)
-    encode(low, high, x, atom_bias, index, cond, enc_project, enc_mix, pool, enc, residual, packed, mixed)
+    x[:, HALO : HALO + inner] = atoms_in[...]
+    packed[:, :, 3 * width :] = jnp.ones((seeds, total, width), BF)
+    mixed[:, :RIM] = jnp.zeros((seeds, RIM, width), BF)
+    mixed[:, total - RIM :] = jnp.zeros((seeds, RIM, width), BF)
+    packed_rows(packed, enc_project, x, HALO, HALO + inner, 256)
+
+    @pl.when(has_below)
+    def _():
+        for part in upward:
+            up(*part).wait_recv()
+
+    @pl.when(has_above)
+    def _():
+        for part in downward:
+            below(*part).wait_recv()
+
+    packed_rows(packed, enc_project, x, 0, HALO, HALO)
+    packed_rows(packed, enc_project, x, HALO + inner, total, HALO)
+    low = jnp.where(tok == 0, HALO, 0)
+    high = jnp.where(tok == count - 1, HALO + inner, total)
+    loads[6].wait()
+    blocks = inner // QUERY_BLOCK
+    rim_blocks = 2 * RIM // QUERY_BLOCK
+    window_attention(packed, atom_bias, mixed, HALO - RIM, blocks + rim_blocks, low, high, 2)
+    index = jnp.concatenate([low_index[:1], index_in[...], high_index[:1]], axis=1)
+    index = index - tok * inner_tokens
+    pool_tokens(x, index, cond, enc_mix, pool, enc, residual, mixed)
 
     tokens, width = cond.shape
     everyone[tok] = layer_norm(residual[...]).astype(BF)
@@ -318,7 +398,53 @@
     loads[4].wait()
     state = (state + mm(part, down[...])).astype(BF)
     state_out[...] = state.reshape(seeds, tokens, width)
-    spread_out[...] = mm(state, spread_w[...]).astype(BF).reshape(spread_out.shape)
+    part = mm(state, spread_w[...]).astype(BF)
+    spread[:, EDGE : EDGE + tokens] = part.reshape(seeds, tokens, part.shape[1])
+
+    @pl.when(has_above)
+    def _():
+        up(*edge_up).start()
+
+    @pl.when(has_below)
+    def _():
+        below(*edge_down).start()
+
+    @pl.when(has_below)
+    def _():
+        up(*edge_up).wait_recv()
+
+    @pl.when(has_above)
+    def _():
+        below(*edge_down).wait_recv()
+
+    picker = (index == iota((tokens + 2 * EDGE, total), 0) - EDGE).astype(BF)
+    for s in range(seeds):
+        for at in range(0, total, 256):
+            carried = lax.dot_general(
+                picker[:, at : at + 256], spread[s], (((0,), (0,)), ((), ())),
+                preferred_element_type=F32,
+            )
+            decoded[s, at : at + 256, :] = (
+                enc[s, at : at + 256, :].astype(F32) + carried
+            ).astype(BF)
+    packed_rows(packed, dec_project, decoded, 0, total, 256)
+    loads[5].wait()
+    window_attention(packed, dec_bias, mixed, HALO, blocks, low, high, 2)
+    for s in range(seeds):
+        for at in range(HALO, HALO + inner, 256):
+            base = decoded[s, at : at + 256, :].astype(F32)
+            part = base + mm(mixed[s, at : at + 256, :], dec_mix[...])
+            out[s, at - HALO : at - HALO + 256, :] = part.astype(BF)
+
+    @pl.when(has_above)
+    def _():
+        for part in upward + [edge_up]:
+            up(*part).wait_send()
+
+    @pl.when(has_below)
+    def _():
+        for part in downward + [edge_down]:
+            below(*part).wait_send()
 
     to_twin(0).wait_send()
     for k in range(hops):
@@ -338,40 +464,6 @@
         @pl.when(chip + k + 1 < chips)
         def _(k=k):
             to_twin(k + 1).wait_send()
-
-
-def decode_kernel(count, enc, spread, index, bias, project, mix, out, decoded, packed, mixed):
-    seeds, rows, width = enc.shape
-    inner = out.shape[1]
-    low, high = limits(lax.axis_index("tok"), count, RIM, inner, rows)
-    picker = (index[...] == iota((spread.shape[1], rows), 0) - EDGE).astype(BF)
-    chunk = rows // 3
-    for s in range(seeds):
-        for at in range(0, rows, chunk):
-            carried = lax.dot_general(
-                picker[:, at : at + chunk], spread[s], (((0,), (0,)), ((), ())),
-                preferred_element_type=F32,
-            )
-            part = (enc[s, at : at + chunk, :].astype(F32) + carried).astype(BF)
-            decoded[s, at : at + chunk, :] = part
-            part = layer_norm(part.astype(F32)).astype(BF)
-            packed[s, at : at + chunk, : 3 * width] = mm(part, project[...]).astype(BF)
-    packed[:, :, 3 * width :] = jnp.ones((seeds, rows, width), BF)
-    window_attention(packed, bias, mixed, inner // QUERY_BLOCK, RIM - 48, low, high, 2)
-    for s in range(seeds):
-        for at in range(0, inner, 256):
-            base = decoded[s, RIM + at : RIM + at + 256, :].astype(F32)
-            out[s, at : at + 256, :] = (base + mm(mixed[s, at : at + 256, :], mix[...])).astype(BF)
-
-
-PARAMS = pltpu.CompilerParams(vmem_limit_bytes=50 * 1024 * 1024)
-
-
-def exchange(to_above, to_below):
-    count = lax.axis_size("tok")
-    above = [(i, i + 1) for i in range(count - 1)]
-    below = [(target, source) for source, target in above]
-    return lax.ppermute(to_above, "tok", above), lax.ppermute(to_below, "tok", below)
 
 
 def per_device(
@@ -383,8 +475,6 @@
     tokens, token_width = token_cond.shape
     atom_heads, window = atom_bias_enc.shape[1:]
     count = lax.axis_size("tok")
-    tok = lax.axis_index("tok")
-    relative = atom_index - tok * tokens
     x = atom_feats.transpose(1, 0, 2)
 
     def by_head(bias):
@@ -394,53 +484,33 @@
     enc_bias = by_head(atom_bias_enc)
     dec_bias = by_head(atom_bias_dec)
 
-    def parcel(at, at_rim):
-        row = jnp.zeros((8, width), BF).at[0, :RIM].set(relative[at_rim : at_rim + RIM].astype(BF))
-        rim = atom_heads * at_rim
-        return jnp.concatenate(
-            [
-                x[:, at : at + HALO].reshape(seeds * HALO, width),
-                enc_bias[rim : rim + atom_heads * RIM],
-                row,
-            ]
-        )
-
-    def unpack(parcel):
-        cut = seeds * HALO
-        end = cut + atom_heads * RIM
-        return (
-            parcel[:cut].reshape(seeds, HALO, width),
-            parcel[cut:end],
-            parcel[end, :RIM].astype(jnp.int32),
-        )
-
-    lower, upper = exchange(parcel(atoms - HALO, atoms - RIM), parcel(0, 0))
-    lower_x, lower_bias, lower_index = unpack(lower)
-    upper_x, upper_bias, upper_index = unpack(upper)
-    x_ext = jnp.concatenate([lower_x, x, upper_x], axis=1)
-    bias_ext = jnp.concatenate([lower_bias, enc_bias, upper_bias])
-    lower_index = jnp.where(tok == 0, MISSING, lower_index - tokens)
-    upper_index = jnp.where(tok == count - 1, MISSING, upper_index + tokens)
-    index_ext = jnp.concatenate([lower_index, relative, upper_index])[None]
-    rows = atoms + 2 * RIM
-
+    first_index = jnp.broadcast_to(atom_index[None, :HALO], (8, HALO))
+    last_index = jnp.broadcast_to(atom_index[None, atoms - HALO :], (8, HALO))
+    total = atoms + 2 * HALO
     groups = lax.axis_size("seed")
     hops = max(count // 2 - 1, 1)
     vmem = pl.BlockSpec(memory_space=pltpu.VMEM)
     hbm = pl.BlockSpec(memory_space=pl.ANY)
     flat = (seeds, tokens, token_width)
     dma = pltpu.SemaphoreType.DMA
-    encoded, state, spread = pl.pallas_call(
+    state, update = pl.pallas_call(
         functools.partial(main_kernel, count, groups),
         out_shape=(
-            jax.ShapeDtypeStruct((seeds, rows, width), BF),
             jax.ShapeDtypeStruct(flat, BF),
-            jax.ShapeDtypeStruct((seeds, tokens, width), BF),
+            jax.ShapeDtypeStruct((seeds, atoms, width), BF),
         ),
-        in_specs=[vmem] * 7 + [hbm] * 5 + [vmem],
+        in_specs=[vmem, hbm] + [vmem] * 7 + [hbm] * 5 + [vmem, hbm, vmem, vmem],
         scratch_shapes=[
-            pltpu.VMEM((seeds, atoms + 2 * HALO, 4 * width), BF),
-            pltpu.VMEM((seeds, rows, width), BF),
+            pltpu.VMEM((seeds, total, width), BF),
+            pltpu.VMEM(((atoms + 2 * RIM) * atom_heads, window), BF),
+            pltpu.VMEM((8, HALO), jnp.int32),
+            pltpu.VMEM((8, HALO), jnp.int32),
+            pltpu.VMEM((seeds, total, width), BF),
+            pltpu.VMEM((seeds, total, width), BF),
+            pltpu.VMEM((seeds, tokens + 2 * EDGE, width), BF),
+            pltpu.VMEM(dec_bias.shape, BF),
+            pltpu.VMEM((seeds, total, 4 * width), BF),
+            pltpu.VMEM((seeds, total, width), BF),
             pltpu.VMEM(flat, F32),
             pltpu.VMEM((count,) + flat, BF),
             pltpu.VMEM((seeds, count * tokens, 2 * token_width), BF),
@@ -452,7 +522,7 @@
             pltpu.VMEM(token_mix.shape, BF),
             pltpu.VMEM(swiglu_in.shape, BF),
             pltpu.VMEM(swiglu_out.shape, BF),
-            dma((5,)),
+            dma((7,)),
             dma((groups - 1,)),
             dma((groups - 1,)),
             dma((hops,)),
@@ -461,27 +531,18 @@
             dma((hops,)),
             dma((2 * hops + 1,)),
             dma((2 * hops + 1,)),
+            dma((4,)),
+            dma((4,)),
+            dma((4,)),
+            dma((4,)),
         ],
         compiler_params=pltpu.CompilerParams(
-            vmem_limit_bytes=56 * 1024 * 1024, collective_id=0, has_side_effects=True
+            vmem_limit_bytes=60 * 1024 * 1024, collective_id=0, has_side_effects=True
         ),
         name="main",
-    )(x_ext, bias_ext, index_ext, token_cond, enc_project, enc_mix, pool_weight, pair_bias,
-      token_project, token_mix, swiglu_in, swiglu_out, spread_weight)
-
-    low_rows, high_rows = exchange(spread[:, tokens - EDGE :], spread[:, :EDGE])
-    spread_ext = jnp.concatenate([low_rows, spread, high_rows], axis=1)
-    update = pl.pallas_call(
-        functools.partial(decode_kernel, count),
-        out_shape=jax.ShapeDtypeStruct((seeds, atoms, width), BF),
-        scratch_shapes=[
-            pltpu.VMEM((seeds, rows, width), BF),
-            pltpu.VMEM((seeds, rows, 4 * width), BF),
-            pltpu.VMEM((seeds, atoms, width), BF),
-        ],
-        compiler_params=PARAMS,
-        name="decode",
-    )(encoded, spread_ext, index_ext, dec_bias, dec_project, dec_mix)
+    )(x, enc_bias, atom_index[None], first_index, last_index, token_cond, enc_project, enc_mix,
+      pool_weight, pair_bias, token_project, token_mix, swiglu_in, swiglu_out, spread_weight,
+      dec_bias, dec_project, dec_mix)
     return state.transpose(1, 0, 2), update.transpose(1, 0, 2)
 
 

time: 104 us -> 95.9 us (0.922)
  starting transfers between devices: 11.7 us -> 0 us
  local copies, waits for them, and re-layouts: 5.77 us -> 13.3 us
  waiting for transfers between devices: 5.9 us -> 0 us
  Pallas kernels: 76.5 us -> 80.9 us
  other arithmetic: 2.8 us -> 0 us
    pallas_call x1, Pallas kernels: 65.9 us -> 80.9 us  [per_device(): pl.pallas_call(functools.partial(main_kernel, count, groups), out_shape=(...]
    ppermute x4 -> x0, starting transfers between devices: 11.7 us -> none  [the longest x2 7.81 us: exchange(): lax.ppermute(to_above, 'tok', above)]
    pallas_call x1 -> x0, Pallas kernels: 10.6 us -> none  [per_device(): pl.pallas_call(functools.partial(decode_kernel, count), out_shape=jax.Sha...]
    ppermute x4 -> x0, waiting for transfers between devices: 5.9 us -> none  [the longest x2 5.9 us: exchange(): lax.ppermute(to_below, 'tok', below)]
    unnamed x19 -> x3, local copies, waits for them, and re-layouts: 2.59 us -> 6.42 us
    reshape x2, local copies, waits for them, and re-layouts: 1.64 us -> 4.9 us  [by_head(): parts = bias.reshape(atoms // QUERY_BLOCK, QUERY_BLOCK, atom_heads, window)]
    concatenate x5 -> x0, other arithmetic: 2.04 us -> none  [the longest x1 1.13 us: per_device(): bias_ext = jnp.concatenate([lower_bias, enc_bias, upper_bias])]
  transfers between devices with their start and end apart: 4 -> 0, of which waited for: 2 -> 0; matrix products, arithmetic and copies ran while one was open for 1% -> 0% of each run, Pallas kernels for 0% -> 0%
where the time goes in v3:
time: 95.9 us; the launch traced here: 94.8 us
  Pallas kernels  80.9 us (84%)
  local copies, waits for them, and re-layouts  13.3 us (14%)
    pallas_call x1, Pallas kernels, per_device(): pl.pallas_call(functools.partial(main_kernel, count, groups), out_shape=(...  80.9 us
    unnamed x3, local copies, waits for them, and re-layouts  6.42 us
    reshape x2, local copies, waits for them, and re-layouts, by_head(): parts = bias.reshape(atoms // QUERY_BLOCK, QUERY_BLOCK, atom_heads, window)  4.9 us

profile of v3, /device:TPU:1, one launch (start us, length us, event | category | flops | bytes accessed | tf_op | source)
XLA Modules:
  0.0 94.8 jit_solution(12361796540269532718)
XLA Ops:
  0.6 0.8 fusion
  1.4 0.6 broadcast_in_dim.8.last_index
  2.0 0.6 broadcast_in_dim.7.first_index
  2.6 1.9 %copy.24 = bf16[1024,2,128]{2,0,1:T(8,128)(2,1)} copy(bf16[1024,2,128]{2,1,0:T(2,128)(2,1)} %param.16) | data formatting | bytes 1048576 | tf_op args[0]
  4.5 2.4 %copy.19 = bf16[32,32,4,128]{3,1,2,0:T(8,128)(2,1)} copy(bf16[32,32,4,128]{3,2,1,0:T(4,128)(2,1)} %bitcast.17) | data formatting | bytes 2097152 | tf_op jit(solution)/shard_map/reshape | solution.py:481
  6.9 2.5 %copy.20 = bf16[32,32,4,128]{3,1,2,0:T(8,128)(2,1)} copy(bf16[32,32,4,128]{3,2,1,0:T(4,128)(2,1)} %bitcast.18) | data formatting | bytes 2097152 | tf_op jit(solution)/shard_map/reshape | solution.py:481
  9.4 80.9 %main.1 = (bf16[2,128,768]{2,1,0:T(8,128)(2,1)}, bf16[2,1024,128]{2,1,0:T(8,128)(2,1)}) custom-call(bf16[2,1024,128]{2,1,0:T(8,128)(2,1)} %bitcast.16, bf16[4096,128]{1,0:T(8,128)(2,1)} %bitcast.14, s32[1,1024]{1,0:T(1,128)} %bitcast.21, s32[8,128]{1,0:T(8,128)} %broadcast_in_dim.7.first_index, s32[8,128]{1,0:T(8,128)} %broadcast_in_dim.8.last_index, ...), custom_call_target="tpu_custom_call" | custom-call | tf_op jit(solution)/shard_map/main/pallas_call | solution.py:496
  90.3 2.1 %copy.21 = bf16[128,2,768]{2,1,0:T(2,128)(2,1)} copy(bf16[128,2,768]{2,0,1:T(8,128)(2,1)} %bitcast.20) | data formatting | bytes 786432
  92.4 2.4 %copy.22 = bf16[1024,2,128]{2,1,0:T(2,128)(2,1)} copy(bf16[1024,2,128]{2,0,1:T(8,128)(2,1)} %bitcast.19) | data formatting | bytes 1048576

commit v4 on v3

--- a/solution.py
+++ b/solution.py
@@ -47,13 +47,16 @@
     margin = (window - QUERY_BLOCK) // 2
     column = iota((QUERY_BLOCK, width), 1) // size
     lane = iota((rows, window), 1)
+    row, source = iota((rows, rows), 0), iota((rows, rows), 1)
+    order = (source // heads == row % QUERY_BLOCK) & (source % heads == row // QUERY_BLOCK)
+    order = order.astype(BF)
 
     def step(i, carry):
         scores, places = [], []
         for g in range(group):
             j = i * group + g
             start = pl.multiple_of(first_row - margin + QUERY_BLOCK * j, 16)
-            term = bias[pl.ds(pl.multiple_of(rows * j, rows), rows), :].astype(F32)
+            term = mm(order, bias[pl.ds(pl.multiple_of(rows * j, rows), rows), :])
             spot = lane + start
             term = jnp.where((spot >= low) & (spot < high), term, NEGATIVE)
             for s in range(seeds):
@@ -109,37 +112,79 @@
         residual[s] = cond[...].astype(F32) + sums / counts
 
 
-def attend(bias, query, kv, attended):
+def head_lanes(size, h, rows):
+    first = size * h // 128
+    last = (size * h + size - 1) // 128
+    spot = iota((rows, (last - first + 1) * 128), 1) + first * 128
+    return first, last, (spot >= size * h) & (spot < size * (h + 1))
+
+
+def attend(first_key, bias, query, kv, attended, tops, sums):
     seeds, tokens, width = query.shape
+    keys_here = 2 * tokens
     heads = bias.shape[0]
     size = width // heads
     span = 384
     group = span // size
+    where = pl.ds(pl.multiple_of(first_key, keys_here), keys_here)
 
     def step(i, carry):
         s = i // (heads // group)
         g = i % (heads // group)
         left = pl.multiple_of(g * span, 128)
-        tiles = [jnp.zeros((tokens, 128), F32) for _ in range(span // 128)]
+        tiles = [
+            attended[s, :, pl.ds(pl.multiple_of(left + t * 128, 128), 128)]
+            for t in range(span // 128)
+        ]
         for h in range(group):
-            first = size * h // 128
-            last = (size * h + size - 1) // 128
-            wide_here = (last - first + 1) * 128
-            lanes = pl.ds(pl.multiple_of(left + first * 128, 128), wide_here)
-            spot = iota((tokens, wide_here), 1) + first * 128
-            mine = (spot >= size * h) & (spot < size * (h + 1))
+            first, last, mine = head_lanes(size, h, tokens)
+            wide = (last - first + 1) * 128
+            lanes = pl.ds(pl.multiple_of(left + first * 128, 128), wide)
             q = query[s, :, lanes]
             q = jnp.where(mine, q, jnp.zeros_like(q))
-            keys = kv[s, :, lanes]
-            values = kv[s, :, pl.ds(pl.multiple_of(left + width + first * 128, 128), wide_here)]
-            scores = mm_t(q, keys) * size ** (-0.5) + bias[g * group + h].astype(F32)
-            weights = jnp.exp(scores - jnp.max(scores, axis=-1, keepdims=True))
-            sums = jnp.sum(weights, axis=-1, keepdims=True)
-            part = jnp.where(mine, mm(weights.astype(BF), values) / sums, 0.0)
+            keys = kv[:, s, :, lanes].reshape(keys_here, wide)
+            values = kv[:, s, :, pl.ds(pl.multiple_of(left + width + first * 128, 128), wide)]
+            scores = mm_t(q, keys) * size ** (-0.5) + bias[g * group + h, :, where].astype(F32)
+            spot = s * heads + g * group + h
+            before = tops[spot]
+            top = jnp.maximum(before, jnp.max(scores, axis=-1, keepdims=True))
+            shrink = jnp.exp(before - top)
+            weights = jnp.exp(scores - jnp.concatenate([top] * (keys_here // 128), axis=1))
+            total = sums[spot] * shrink
+            for at in range(0, keys_here, 128):
+                total = total + weights[:, at : at + 128]
+            tops[spot] = top
+            sums[spot] = total
+            part = mm(weights.astype(BF), values.reshape(keys_here, wide))
             for t in range(first, last + 1):
-                tiles[t] = tiles[t] + part[:, (t - first) * 128 : (t - first + 1) * 128]
+                here = slice((t - first) * 128, (t - first + 1) * 128)
+                tiles[t] = jnp.where(mine[:, here], tiles[t] * shrink + part[:, here], tiles[t])
         for t, tile in enumerate(tiles):
             attended[s, :, pl.ds(pl.multiple_of(left + t * 128, 128), 128)] = tile
+        return carry
+
+    lax.fori_loop(0, seeds * (heads // group), step, 0)
+
+
+def settle(heads, attended, sums):
+    seeds, tokens, width = attended.shape
+    size = width // heads
+    span = 384
+    group = span // size
+
+    def step(i, carry):
+        s = i // (heads // group)
+        g = i % (heads // group)
+        tiles = [jnp.ones((tokens, 128), F32) for _ in range(span // 128)]
+        for h in range(group):
+            first, last, mine = head_lanes(size, h, tokens)
+            total = jnp.sum(sums[s * heads + g * group + h], axis=-1, keepdims=True)
+            for t in range(first, last + 1):
+                here = slice((t - first) * 128, (t - first + 1) * 128)
+                tiles[t] = jnp.where(mine[:, here], total, tiles[t])
+        for t, tile in enumerate(tiles):
+            lanes = pl.ds(pl.multiple_of(g * span + t * 128, 128), 128)
+            attended[s, :, lanes] = attended[s, :, lanes] / tile
         return carry
 
     lax.fori_loop(0, seeds * (heads // group), step, 0)
@@ -154,11 +199,11 @@
 
 def main_kernel(
     count, groups,
-    atoms_in, enc_bias_hbm, index_in, first_index, last_index, cond, enc_project, enc_mix, pool,
+    atoms_in, enc_bias_hbm, index_in, cond, enc_project, enc_mix, pool,
     bias_hbm, project_hbm, mix_hbm, wide_hbm, down_hbm, spread_w, dec_bias_hbm, dec_project, dec_mix,
     state_out, out,
     x, atom_bias, low_index, high_index, enc, decoded, spread, dec_bias,
-    packed, mixed, residual, everyone, kv, query, gate, attended, bias, project, mix, wide, down,
+    packed, mixed, residual, everyone, kv, query, gate, attended, tops, sums, bias, project, mix, wide, down,
     sems, bias_send, bias_recv, right_send, right_recv, left_send, left_recv, twin_send, twin_recv,
     up_send, up_recv, down_send, down_recv,
 ):
@@ -200,8 +245,19 @@
     has_right = jnp.where(chip < chips - 1, 1, 0)
     pl.semaphore_wait(barrier, groups + has_left + has_right + jnp.where(has_side, 1, 0))
 
-    seeds, inner, width = atoms_in.shape
-    total = inner + 2 * HALO
+    seeds, total, width = x.shape
+    inner = total - 2 * HALO
+    turn = seeds * HALO
+    row, source = iota((turn, turn), 0), iota((turn, turn), 1)
+    split = (source == seeds * (row % HALO) + row // HALO).astype(BF)
+
+    def take_in(at):
+        part = mm(split, atoms_in[seeds * at : seeds * (at + HALO), :]).astype(BF)
+        for s in range(seeds):
+            x[s, HALO + at : 2 * HALO + at, :] = part[s * HALO : (s + 1) * HALO]
+
+    take_in(0)
+    take_in(inner - HALO)
     heads = enc_bias_hbm.shape[0] // inner
     rim = heads * RIM
     own_bias = heads * inner
@@ -215,14 +271,14 @@
         return remote(source, target, down_send.at[i], down_recv.at[i], tok=tok - 1)
 
     upward = [
-        (0, atoms_in.at[:, pl.ds(inner - HALO, HALO)], x.at[:, pl.ds(0, HALO)]),
+        (0, x.at[:, pl.ds(inner, HALO)], x.at[:, pl.ds(0, HALO)]),
         (1, enc_bias_hbm.at[pl.ds(own_bias - rim, rim)], atom_bias.at[pl.ds(0, rim)]),
-        (2, last_index, low_index),
+        (2, index_in, low_index),
     ]
     downward = [
-        (0, atoms_in.at[:, pl.ds(0, HALO)], x.at[:, pl.ds(HALO + inner, HALO)]),
+        (0, x.at[:, pl.ds(HALO, HALO)], x.at[:, pl.ds(HALO + inner, HALO)]),
         (1, enc_bias_hbm.at[pl.ds(0, rim)], atom_bias.at[pl.ds(rim + own_bias, rim)]),
-        (2, first_index, high_index),
+        (2, index_in, high_index),
     ]
     edge_up = (3, spread.at[:, pl.ds(inner_tokens, EDGE)], spread.at[:, pl.ds(0, EDGE)])
     edge_down = (3, spread.at[:, pl.ds(EDGE, EDGE)], spread.at[:, pl.ds(EDGE + inner_tokens, EDGE)])
@@ -253,13 +309,28 @@
 
     share = bias_hbm.shape[0]
     slot = bias.at[pl.ds(seed * share, share)]
-    bias_copies = [
-        remote(bias_hbm, slot, bias_send.at[k - 1], bias_recv.at[k - 1],
-               seed=lax.rem(seed + k, groups))
-        for k in range(1, groups)
-    ]
-    for copy in bias_copies:
-        copy.start()
+    both = jnp.minimum(chip, chips - 1 - chip)
+
+    def offset(p):
+        near = (p + 1) // 2
+        inside = jnp.where(p % 2 == 1, -near, near)
+        outside = jnp.where(chip > chips - 1 - chip, both - p, p - both)
+        return jnp.where(p <= 2 * both, inside, outside)
+
+    def event(k):
+        return jnp.where(k <= both + 1, max(1, 2 * (k - 1)), both + k)
+
+    def bias_copy(k, p):
+        first = pl.multiple_of((chip + offset(p)) * (2 * inner_tokens), 2 * inner_tokens)
+        lanes = pl.ds(first, 2 * inner_tokens)
+        return remote(
+            bias_hbm.at[:, :, lanes], bias.at[pl.ds(seed * share, share), :, lanes],
+            bias_send.at[k - 1, p], bias_recv.at[k - 1, p], seed=lax.rem(seed + k, groups),
+        )
+
+    for p in range(chips):
+        for k in range(1, groups):
+            bias_copy(k, p).start()
     loads = [
         pltpu.make_async_copy(source, target, sems.at[i])
         for i, (source, target) in enumerate(
@@ -273,7 +344,8 @@
     for load in loads:
         load.start()
 
-    x[:, HALO : HALO + inner] = atoms_in[...]
+    for at in range(HALO, inner - HALO, HALO):
+        take_in(at)
     packed[:, :, 3 * width :] = jnp.ones((seeds, total, width), BF)
     mixed[:, :RIM] = jnp.zeros((seeds, RIM, width), BF)
     mixed[:, total - RIM :] = jnp.zeros((seeds, RIM, width), BF)
@@ -297,7 +369,12 @@
     blocks = inner // QUERY_BLOCK
     rim_blocks = 2 * RIM // QUERY_BLOCK
     window_attention(packed, atom_bias, mixed, HALO - RIM, blocks + rim_blocks, low, high, 2)
-    index = jnp.concatenate([low_index[:1], index_in[...], high_index[:1]], axis=1)
+    index = jnp.concatenate(
+        [low_index[inner // HALO - 1 :]]
+        + [index_in[i : i + 1] for i in range(inner // HALO)]
+        + [high_index[:1]],
+        axis=1,
+    )
     index = index - tok * inner_tokens
     pool_tokens(x, index, cond, enc_mix, pool, enc, residual, mixed)
 
@@ -331,62 +408,47 @@
     query[...] = mm(own, project[:, :width]).astype(BF).reshape(seeds, tokens, width)
     gate[...] = jax.nn.sigmoid(mm(own, project[:, 3 * width :]))
 
-    def keys_values(place):
-        part = everyone[place].reshape(seeds * tokens, width)
-        first = pl.multiple_of(place * tokens, tokens)
+    attended[...] = jnp.zeros(attended.shape, F32)
+    sums[...] = jnp.zeros(sums.shape, F32)
+    tops[...] = jnp.full(tops.shape, NEGATIVE, F32)
+    loads[0].wait()
+
+    def visit(p, carry):
+        for k in range(1, hops + 1):
+
+            @pl.when((p == event(k)) & (chip - k >= 0))
+            def _(k=k):
+                to_right(k - 1).wait_recv()
+                to_twin(-k).start()
+                if k < hops:
+
+                    @pl.when(chip < chips - 1)
+                    def _():
+                        to_right(k).start()
+
+            @pl.when((p == event(k)) & (chip + k < chips))
+            def _(k=k):
+                to_left(k - 1).wait_recv()
+                to_twin(k).start()
+                if k < hops:
+
+                    @pl.when(chip > 0)
+                    def _():
+                        to_left(k).start()
+
+        away = offset(p)
+        to_twin(away).wait_recv()
+        part = everyone[pl.ds(2 * (chip + away), 2)].reshape(2 * seeds * tokens, width)
         for at in range(0, 2 * width, width):
             piece = mm(part, project[:, width + at : 2 * width + at]).astype(BF)
-            kv[:, pl.ds(first, tokens), at : at + width] = piece.reshape(seeds, tokens, width)
-
-    keys_values(tok)
-    to_twin(0).wait_recv()
-    keys_values(twin)
-    for k in range(1, hops + 1):
-        from_left = chip - k >= 0
-        from_right = chip + k < chips
-
-        @pl.when(from_left)
-        def _(k=k):
-            to_right(k - 1).wait_recv()
-            to_twin(-k).start()
-            if k < hops:
-
-                @pl.when(chip < chips - 1)
-                def _():
-                    to_right(k).start()
-
-        @pl.when(from_right)
-        def _(k=k):
-            to_left(k - 1).wait_recv()
-            to_twin(k).start()
-            if k < hops:
-
-                @pl.when(chip > 0)
-                def _():
-                    to_left(k).start()
-
-        @pl.when(from_left)
-        def _(k=k):
-            keys_values(tok - 2 * k)
-
-        @pl.when(from_right)
-        def _(k=k):
-            keys_values(tok + 2 * k)
-
-        @pl.when(from_left)
-        def _(k=k):
-            to_twin(-k).wait_recv()
-            keys_values(twin - 2 * k)
-
-        @pl.when(from_right)
-        def _(k=k):
-            to_twin(k).wait_recv()
-            keys_values(twin + 2 * k)
-
-    loads[0].wait()
-    for copy in bias_copies:
-        copy.wait()
-    attend(bias, query, kv, attended)
+            kv[:, :, :, at : at + width] = piece.reshape(2, seeds, tokens, width)
+        for k in range(1, groups):
+            bias_copy(k, p).wait_recv()
+        attend((chip + away) * (2 * tokens), bias, query, kv, attended, tops, sums)
+        return carry
+
+    lax.fori_loop(0, chips, visit, 0)
+    settle(bias.shape[0], attended, sums)
 
     loads[2].wait()
     gated = (attended[...].reshape(seeds * tokens, width) * gate[...]).astype(BF)
@@ -447,6 +509,9 @@
             below(*part).wait_send()
 
     to_twin(0).wait_send()
+    for p in range(chips):
+        for k in range(1, groups):
+            bias_copy(k, p).wait_send()
     for k in range(hops):
 
         @pl.when((chip - k >= 0) & (chip < chips - 1))
@@ -475,17 +540,11 @@
     tokens, token_width = token_cond.shape
     atom_heads, window = atom_bias_enc.shape[1:]
     count = lax.axis_size("tok")
-    x = atom_feats.transpose(1, 0, 2)
-
-    def by_head(bias):
-        parts = bias.reshape(atoms // QUERY_BLOCK, QUERY_BLOCK, atom_heads, window)
-        return parts.transpose(0, 2, 1, 3).reshape(atoms * atom_heads, window)
-
-    enc_bias = by_head(atom_bias_enc)
-    dec_bias = by_head(atom_bias_dec)
-
-    first_index = jnp.broadcast_to(atom_index[None, :HALO], (8, HALO))
-    last_index = jnp.broadcast_to(atom_index[None, atoms - HALO :], (8, HALO))
+    x = atom_feats.reshape(atoms * seeds, width)
+
+    enc_bias = atom_bias_enc.reshape(atoms * atom_heads, window)
+    dec_bias = atom_bias_dec.reshape(atoms * atom_heads, window)
+    index = atom_index.reshape(atoms // HALO, HALO)
     total = atoms + 2 * HALO
     groups = lax.axis_size("seed")
     hops = max(count // 2 - 1, 1)
@@ -499,12 +558,12 @@
             jax.ShapeDtypeStruct(flat, BF),
             jax.ShapeDtypeStruct((seeds, atoms, width), BF),
         ),
-        in_specs=[vmem, hbm] + [vmem] * 7 + [hbm] * 5 + [vmem, hbm, vmem, vmem],
+        in_specs=[vmem, hbm] + [vmem] * 5 + [hbm] * 5 + [vmem, hbm, vmem, vmem],
         scratch_shapes=[
             pltpu.VMEM((seeds, total, width), BF),
             pltpu.VMEM(((atoms + 2 * RIM) * atom_heads, window), BF),
-            pltpu.VMEM((8, HALO), jnp.int32),
-            pltpu.VMEM((8, HALO), jnp.int32),
+            pltpu.VMEM(index.shape, jnp.int32),
+            pltpu.VMEM(index.shape, jnp.int32),
             pltpu.VMEM((seeds, total, width), BF),
             pltpu.VMEM((seeds, total, width), BF),
             pltpu.VMEM((seeds, tokens + 2 * EDGE, width), BF),
@@ -513,18 +572,20 @@
             pltpu.VMEM((seeds, total, width), BF),
             pltpu.VMEM(flat, F32),
             pltpu.VMEM((count,) + flat, BF),
-            pltpu.VMEM((seeds, count * tokens, 2 * token_width), BF),
+            pltpu.VMEM((2, seeds, tokens, 2 * token_width), BF),
             pltpu.VMEM(flat, BF),
             pltpu.VMEM((seeds * tokens, token_width), F32),
             pltpu.VMEM(flat, F32),
+            pltpu.VMEM((seeds * HEADS, tokens, 128), F32),
+            pltpu.VMEM((seeds * HEADS, tokens, 128), F32),
             pltpu.VMEM((HEADS,) + pair_bias.shape[1:], BF),
             pltpu.VMEM(token_project.shape, BF),
             pltpu.VMEM(token_mix.shape, BF),
             pltpu.VMEM(swiglu_in.shape, BF),
             pltpu.VMEM(swiglu_out.shape, BF),
             dma((7,)),
-            dma((groups - 1,)),
-            dma((groups - 1,)),
+            dma((groups - 1, count // 2)),
+            dma((groups - 1, count // 2)),
             dma((hops,)),
             dma((hops,)),
             dma((hops,)),
@@ -540,7 +601,7 @@
             vmem_limit_bytes=60 * 1024 * 1024, collective_id=0, has_side_effects=True
         ),
         name="main",
-    )(x, enc_bias, atom_index[None], first_index, last_index, token_cond, enc_project, enc_mix,
+    )(x, enc_bias, index, token_cond, enc_project, enc_mix,
       pool_weight, pair_bias, token_project, token_mix, swiglu_in, swiglu_out, spread_weight,
       dec_bias, dec_project, dec_mix)
     return state.transpose(1, 0, 2), update.transpose(1, 0, 2)

time: 95.9 us -> 83.4 us (0.87)
  local copies, waits for them, and re-layouts: 13.3 us -> 4.52 us
  Pallas kernels: 80.9 us -> 77 us
    reshape x2 -> x0, local copies, waits for them, and re-layouts: 4.9 us -> none  [by_head(): parts = bias.reshape(atoms // QUERY_BLOCK, QUERY_BLOCK, atom_heads, window)]
    pallas_call x1, Pallas kernels: 80.9 us -> 77 us  [per_device(): pl.pallas_call(functools.partial(main_kernel, count, groups), out_shape=(...]
    unnamed x3 -> x2, local copies, waits for them, and re-layouts: 6.42 us -> 4.52 us
    broadcast_in_dim x2 -> x0, local copies, waits for them, and re-layouts: 1.18 us -> none  [the longest x1 0.59 us: per_device(): first_index = jnp.broadcast_to(atom_index[None, :HALO], (8, HALO))]
where the time goes in v4:
time: 83.4 us; the launch traced here: 82.1 us
  Pallas kernels  77 us (92%)
  local copies, waits for them, and re-layouts  4.52 us (5%)
    pallas_call x1, Pallas kernels, per_device(): pl.pallas_call(functools.partial(main_kernel, count, groups), out_shape=(...  77 us
    unnamed x2, local copies, waits for them, and re-layouts  4.52 us

profile of v4, /device:TPU:1, one launch (start us, length us, event | category | flops | bytes accessed | tf_op | source)
XLA Modules:
  0.0 82.1 jit_solution(8448957438236301622)
XLA Ops:
  0.6 77.0 %main.1 = (bf16[2,128,768]{2,1,0:T(8,128)(2,1)}, bf16[2,1024,128]{2,1,0:T(8,128)(2,1)}) custom-call(bf16[2048,128]{1,0:T(8,128)(2,1)} %bitcast.8, bf16[4096,128]{1,0:T(8,128)(2,1)} %bitcast.6, s32[8,128]{1,0:T(8,128)} %bitcast.11, bf16[128,768]{1,0:T(8,128)(2,1)} %cond.1, bf16[128,384]{1,0:T(8,128)(2,1)} %enc_project.1, bf16[128,128]{1,0:T(8,128)(2,1)} %enc_mix.1, ...), custom_call_target="tpu_custom_call" | custom-call | tf_op jit(solution)/shard_map/main/pallas_call | solution.py:555
  77.6 2.1 %copy.18 = bf16[128,2,768]{2,1,0:T(2,128)(2,1)} copy(bf16[128,2,768]{2,0,1:T(8,128)(2,1)} %bitcast.10) | data formatting | bytes 786432
  79.8 2.4 %copy.19 = bf16[1024,2,128]{2,1,0:T(2,128)(2,1)} copy(bf16[1024,2,128]{2,0,1:T(8,128)(2,1)} %bitcast.9) | data formatting | bytes 1048576

commit v5 on v4

--- a/solution.py
+++ b/solution.py
@@ -328,9 +328,44 @@
             bias_send.at[k - 1, p], bias_recv.at[k - 1, p], seed=lax.rem(seed + k, groups),
         )
 
+    square = groups == 4
+    beside = seed + 1 - 2 * (seed % 2)
+    across = lax.rem(seed + 2, 4)
+
+    def bias_part(i, p, owner, begin, heads_here, target):
+        first = pl.multiple_of((chip + offset(p)) * (2 * inner_tokens), 2 * inner_tokens)
+        lanes = pl.ds(first, 2 * inner_tokens)
+        piece = bias.at[pl.ds(owner * share + begin, heads_here), :, lanes]
+        source = bias_hbm.at[:, :, lanes] if i < 2 else piece
+        return remote(source, piece, bias_send.at[i, p], bias_recv.at[i, p], seed=target)
+
+    def to_neighbours(p):
+        return [bias_part(0, p, seed, 0, share, beside), bias_part(1, p, seed, 0, share, across)]
+
+    def onward(p):
+        half = share // 2
+        return [
+            bias_part(2, p, beside, 0, half, across),
+            bias_part(3, p, across, half, share - half, beside),
+        ]
+
+    def far_copy():
+        first = pl.multiple_of(chip * (2 * inner_tokens), 2 * inner_tokens)
+        lanes = pl.ds(first, 2 * inner_tokens)
+        return remote(
+            bias_hbm.at[:, :, lanes], bias.at[pl.ds(seed * share, share), :, lanes],
+            bias_send.at[2, 0], bias_recv.at[2, 0], seed=3 - seed,
+        )
+
     for p in range(chips):
-        for k in range(1, groups):
-            bias_copy(k, p).start()
+        if square:
+            for copy in to_neighbours(p):
+                copy.start()
+            if p == 0:
+                far_copy().start()
+        else:
+            for k in range(1, groups):
+                bias_copy(k, p).start()
     loads = [
         pltpu.make_async_copy(source, target, sems.at[i])
         for i, (source, target) in enumerate(
@@ -436,14 +471,35 @@
                     def _():
                         to_left(k).start()
 
+        if square:
+
+            @pl.when(p < chips - 1)
+            def _():
+                for copy in to_neighbours(p + 1):
+                    copy.wait_recv()
+                for copy in onward(p + 1):
+                    copy.start()
+
         away = offset(p)
         to_twin(away).wait_recv()
         part = everyone[pl.ds(2 * (chip + away), 2)].reshape(2 * seeds * tokens, width)
         for at in range(0, 2 * width, width):
             piece = mm(part, project[:, width + at : 2 * width + at]).astype(BF)
             kv[:, :, :, at : at + width] = piece.reshape(2, seeds, tokens, width)
-        for k in range(1, groups):
-            bias_copy(k, p).wait_recv()
+        if square:
+
+            @pl.when(p == 0)
+            def _():
+                for copy in to_neighbours(0) + [far_copy()]:
+                    copy.wait_recv()
+
+            @pl.when(p > 0)
+            def _():
+                for copy in onward(p):
+                    copy.wait_recv()
+        else:
+            for k in range(1, groups):
+                bias_copy(k, p).wait_recv()
         attend((chip + away) * (2 * tokens), bias, query, kv, attended, tops, sums)
         return carry
 
@@ -510,8 +566,12 @@
 
     to_twin(0).wait_send()
     for p in range(chips):
-        for k in range(1, groups):
-            bias_copy(k, p).wait_send()
+        if square:
+            for copy in to_neighbours(p) + (onward(p) if p else [far_copy()]):
+                copy.wait_send()
+        else:
+            for k in range(1, groups):
+                bias_copy(k, p).wait_send()
     for k in range(hops):
 
         @pl.when((chip - k >= 0) & (chip < chips - 1))
@@ -584,8 +644,8 @@
             pltpu.VMEM(swiglu_in.shape, BF),
             pltpu.VMEM(swiglu_out.shape, BF),
             dma((7,)),
-            dma((groups - 1, count // 2)),
-            dma((groups - 1, count // 2)),
+            dma((groups, count // 2)),
+            dma((groups, count // 2)),
             dma((hops,)),
             dma((hops,)),
             dma((hops,)),
@@ -598,7 +658,7 @@
             dma((4,)),
         ],
         compiler_params=pltpu.CompilerParams(
-            vmem_limit_bytes=60 * 1024 * 1024, collective_id=0, has_side_effects=True
+            vmem_limit_bytes=50 * 1024 * 1024, collective_id=0, has_side_effects=True
         ),
         name="main",
     )(x, enc_bias, index, token_cond, enc_project, enc_mix,

time: 83.4 us -> 89.2 us (1.070)
  local copies, waits for them, and re-layouts: 4.52 us -> 11.5 us
  Pallas kernels: 77 us -> 75.4 us
    unnamed x2 -> x22, local copies, waits for them, and re-layouts: 4.52 us -> 11.5 us
    pallas_call x1, Pallas kernels: 77 us -> 75.4 us  [per_device(): pl.pallas_call(functools.partial(main_kernel, count, groups), out_shape=(...]
where the time goes in v5:
time: 89.2 us; the launch traced here: 87.6 us
  Pallas kernels  75.4 us (85%)
  local copies, waits for them, and re-layouts  11.5 us (13%)
    pallas_call x1, Pallas kernels, per_device(): pl.pallas_call(functools.partial(main_kernel, count, groups), out_shape=(...  75.4 us
    unnamed x22, local copies, waits for them, and re-layouts  11.5 us

profile of v5, /device:TPU:1, one launch (start us, length us, event | category | flops | bytes accessed | tf_op | source)
XLA Modules:
  0.0 87.6 jit_solution(9571349175041920630)
XLA Ops:
  0.6 0.0 copy-start
  0.6 1.2 %copy-done = bf16[1024,4,128]{2,1,0:T(4,128)(2,1)S(1)} copy-done((bf16[1024,4,128]{2,1,0:T(4,128)(2,1)S(1)}, bf16[1024,4,128]{2,1,0:T(4,128)(2,1)}, u32[]{:S(2)}) %copy-start) | copy-done | bytes 1048600
  1.9 0.0 copy-start.1
  1.9 1.0 %copy-done.1 = bf16[1024,2,128]{2,1,0:T(2,128)(2,1)S(1)} copy-done((bf16[1024,2,128]{2,1,0:T(2,128)(2,1)S(1)}, bf16[1024,2,128]{2,1,0:T(2,128)(2,1)}, u32[]{:S(2)}) %copy-start.1) | copy-done | bytes 524312
  2.9 0.0 copy-start.2
  2.9 0.9 %copy-done.2 = bf16[128,768]{1,0:T(8,128)(2,1)S(1)} copy-done((bf16[128,768]{1,0:T(8,128)(2,1)S(1)}, bf16[128,768]{1,0:T(8,128)(2,1)}, u32[]{:S(2)}) %copy-start.2) | copy-done | bytes 196632
  3.8 0.0 copy-start.3
  3.8 0.9 %copy-done.3 = bf16[128,768]{1,0:T(8,128)(2,1)S(1)} copy-done((bf16[128,768]{1,0:T(8,128)(2,1)S(1)}, bf16[128,768]{1,0:T(8,128)(2,1)}, u32[]{:S(2)}) %copy-start.3) | copy-done | bytes 196632
  4.8 0.0 copy-start.4
  4.8 0.9 %copy-done.4 = bf16[768,128]{1,0:T(8,128)(2,1)S(1)} copy-done((bf16[768,128]{1,0:T(8,128)(2,1)S(1)}, bf16[768,128]{1,0:T(8,128)(2,1)}, u32[]{:S(2)}) %copy-start.4) | copy-done | bytes 196632
  5.7 0.0 copy-start.5
  5.7 0.9 %copy-done.5 = bf16[128,384]{1,0:T(8,128)(2,1)S(1)} copy-done((bf16[128,384]{1,0:T(8,128)(2,1)S(1)}, bf16[128,384]{1,0:T(8,128)(2,1)}, u32[]{:S(2)}) %copy-start.5) | copy-done | bytes 98328
  6.6 0.0 copy-start.6
  6.6 0.9 %copy-done.6 = bf16[128,384]{1,0:T(8,128)(2,1)S(1)} copy-done((bf16[128,384]{1,0:T(8,128)(2,1)S(1)}, bf16[128,384]{1,0:T(8,128)(2,1)}, u32[]{:S(2)}) %copy-start.6) | copy-done | bytes 98328
  7.5 0.0 copy-start.7
  7.5 0.8 copy-done.7
  8.2 0.0 copy-start.8
  8.2 0.8 copy-done.8
  9.0 0.0 copy-start.9
  9.0 0.7 copy-done.9
  9.7 75.4 %main.1 = (bf16[2,128,768]{2,1,0:T(8,128)(2,1)S(1)}, bf16[2,1024,128]{2,1,0:T(8,128)(2,1)S(1)}) custom-call(bf16[2048,128]{1,0:T(8,128)(2,1)S(1)} %bitcast.7, bf16[4096,128]{1,0:T(8,128)(2,1)S(1)} %bitcast.6, s32[8,128]{1,0:T(8,128)S(1)} %bitcast.10, bf16[128,768]{1,0:T(8,128)(2,1)S(1)} %copy-done.2, bf16[128,384]{1,0:T(8,128)(2,1)S(1)} %copy-done.5, ...), custom_call_target="tpu_custom_call" | custom-call | tf_op jit(solution)/shard_map/main/pallas_call | solution.py:615
  85.1 1.2 %copy.18 = bf16[128,2,768]{2,1,0:T(2,128)(2,1)} copy(bf16[128,2,768]{2,0,1:T(8,128)(2,1)S(1)} %bitcast.9) | data formatting | bytes 786432
  86.3 1.3 %copy.19 = bf16[1024,2,128]{2,1,0:T(2,128)(2,1)} copy(bf16[1024,2,128]{2,0,1:T(8,128)(2,1)S(1)} %bitcast.8) | data formatting | bytes 1048576
Async XLA Ops:
  0.6 1.2 %copy-start = (bf16[1024,4,128]{2,1,0:T(4,128)(2,1)S(1)}, bf16[1024,4,128]{2,1,0:T(4,128)(2,1)}, u32[]{:S(2)}) copy-start(bf16[1024,4,128]{2,1,0:T(4,128)(2,1)} %param.20) | copy-start | bytes 3145732
  1.9 1.0 %copy-start.1 = (bf16[1024,2,128]{2,1,0:T(2,128)(2,1)S(1)}, bf16[1024,2,128]{2,1,0:T(2,128)(2,1)}, u32[]{:S(2)}) copy-start(bf16[1024,2,128]{2,1,0:T(2,128)(2,1)} %param.16) | copy-start | bytes 1572868
  2.9 0.9 %copy-start.2 = (bf16[128,768]{1,0:T(8,128)(2,1)S(1)}, bf16[128,768]{1,0:T(8,128)(2,1)}, u32[]{:S(2)}) copy-start(bf16[128,768]{1,0:T(8,128)(2,1)} %cond.1) | copy-start | bytes 589828
  3.8 0.9 %copy-start.3 = (bf16[128,768]{1,0:T(8,128)(2,1)S(1)}, bf16[128,768]{1,0:T(8,128)(2,1)}, u32[]{:S(2)}) copy-start(bf16[128,768]{1,0:T(8,128)(2,1)} %pool.1) | copy-start | bytes 589828
  4.8 0.9 %copy-start.4 = (bf16[768,128]{1,0:T(8,128)(2,1)S(1)}, bf16[768,128]{1,0:T(8,128)(2,1)}, u32[]{:S(2)}) copy-start(bf16[768,128]{1,0:T(8,128)(2,1)} %spread_w.1) | copy-start | bytes 589828
  5.7 0.9 %copy-start.5 = (bf16[128,384]{1,0:T(8,128)(2,1)S(1)}, bf16[128,384]{1,0:T(8,128)(2,1)}, u32[]{:S(2)}) copy-start(bf16[128,384]{1,0:T(8,128)(2,1)} %enc_project.1) | copy-start | bytes 294916
  6.6 0.9 %copy-start.6 = (bf16[128,384]{1,0:T(8,128)(2,1)S(1)}, bf16[128,384]{1,0:T(8,128)(2,1)}, u32[]{:S(2)}) copy-start(bf16[128,384]{1,0:T(8,128)(2,1)} %dec_project.1) | copy-start | bytes 294916
  7.5 0.8 copy-start.7
  8.2 0.8 copy-start.8
  9.0 0.7 copy-start.9
